TPU v7x, 128 devices: a whole 4x4x4 slice. The times are simulated.
128 devices in a mesh: pre: 8 (over x, core), tp: 16 (over z, y).
Axes of the slice: x: 4, y: 4, z: 4, core: 2. Of those that a mesh axis runs over, the one named last changes fastest.
Arguments:
- latent_rows: float32 [131072, 576], P(('pre', 'tp'))
- index_keys: float32 [131072, 128], P(('pre', 'tp'))
- queries: bfloat16 [2, 32, 128, 576], P(None, 'pre', 'tp')
- index_queries: bfloat16 [2, 32, 64, 128], P(None, 'pre')
- index_gates: bfloat16 [2, 32, 64], P(None, 'pre'), may hold values from 0.14941406 to 1.5
- value_proj: bfloat16 [128, 512, 128], P('tp'), may hold values from -2 to 2
- out_proj: bfloat16 [16384, 7168], P('tp'), may hold values from -0.046875 to 0.046875
- block_rows: int32 [2, 32, 64, 64], P(None, 'pre'), may hold values from 0 to 8191, as said below
- block_owner: int32 [2, 32, 64], P(None, 'pre'), may hold values from 0 to 15, as said below
- block_count: int32 [2, 32, 64], P(None, 'pre'), may hold values from 0 to 64, as said below
Outputs:
- attended: bfloat16 [2, 32, 7168], P(None, 'pre')
- index_total: float32 [2, 32], P(None, 'pre')
Inputs may be any that keep to these rules, and one draw needn't show every extreme that they name: `block_owner`: for each step and query every owner is named by exactly 4 blocks. `block_count`: the counts of one step and query sum to 2048; the blocks of one owner hold at most 256 valid rows, and in every step and query some owner holds exactly that many. `block_rows`: rows index the owner's 8192 cache rows; the first block_count entries of a block are valid; the valid rows of one owner in one step and query are distinct.
All inputs are finite; a program needn't handle non-finite values.
Results may differ from a plain program's by a relative error of at most 0.012.
The roundings to bfloat16 on the way count: a program that leaves them out, or rounds other values in their place, can miss the bound.
Values may be sent and summed in bfloat16 or wider, within the bound.
No kernel may reach another device: no remote copies, remote signals or barrier semaphores. Data moves between devices by JAX's collectives and lax.ppermute only.
A program may use at most 128 MiB of HBM per device.

v0:
```python
import jax
import jax.numpy as jnp
from jax import lax
from jax.experimental import pallas as pl
from jax.experimental.pallas import tpu as pltpu
from jax.sharding import PartitionSpec as P

IDX = 128
LAT = 512
KV = 576
BLOCK = 64
PRE = 8
TP = 16
PAIRS = 8
HEADS = 8
ROWS = 1024
HALF = 512
PACK = 256
QTILE = 256
PIECES = 4
STAT = 128
QROWS = TP * PAIRS * HEADS
LOWEST = -3.0e38
SOFT_SCALE = 192.0 ** (-0.5)
LOG2E = 1.4426950408889634
SCORE_SCALE = SOFT_SCALE * LOG2E

NT = (((1,), (1,)), ((), ()))


def vmem():
    return pl.BlockSpec(memory_space=pltpu.VMEM)


def smem():
    return pl.BlockSpec(memory_space=pltpu.SMEM)


def table_kernel(rows_ref, mask_ref, pos_ref, count_ref):
    entries = rows_ref.shape[1]
    high_iota = lax.broadcasted_iota(jnp.int32, (PRE * 8, entries), 0)
    low_iota = lax.broadcasted_iota(jnp.int32, (128, entries), 0)
    for pair in range(PAIRS):
        rows = rows_ref[pair : pair + 1, :]
        high = jnp.where(high_iota == (rows >> 7), 1.0, 0.0).astype(jnp.bfloat16)
        low = jnp.where(low_iota == (rows & 127), 1.0, 0.0).astype(jnp.bfloat16)
        chosen = lax.dot_general(high, low, NT, preferred_element_type=jnp.float32)
        for block in range(PRE):
            for part in range(8):
                mask_ref[block, pair : pair + 1, part * 128 : (part + 1) * 128] = chosen[
                    block * 8 + part : block * 8 + part + 1, :
                ]
    union = jnp.concatenate([jnp.max(mask_ref[block], axis=0, keepdims=True) for block in range(PRE)], axis=0)
    before = (
        lax.broadcasted_iota(jnp.int32, (128, 128), 0) < lax.broadcasted_iota(jnp.int32, (128, 128), 1)
    ).astype(jnp.float32).astype(jnp.bfloat16)
    carry = jnp.zeros((PRE, 1), jnp.float32)
    for part in range(8):
        piece = union[:, part * 128 : (part + 1) * 128]
        ahead = jnp.dot(piece.astype(jnp.bfloat16), before, preferred_element_type=jnp.float32) + carry
        pos_ref[:, part * 128 : (part + 1) * 128] = jnp.where(piece > 0.0, ahead, -1.0)
        carry = carry + jnp.sum(piece, axis=1, keepdims=True)
    count_ref[...] = jnp.broadcast_to(carry, (PRE, 128)).astype(jnp.int32)


def make_tables(effective_rows):
    return pl.pallas_call(
        table_kernel,
        out_shape=(
            jax.ShapeDtypeStruct((PRE, PAIRS, ROWS), jnp.float32),
            jax.ShapeDtypeStruct((PRE, ROWS), jnp.float32),
            jax.ShapeDtypeStruct((PRE, 128), jnp.int32),
        ),
        in_specs=[vmem()],
        out_specs=(vmem(), vmem(), vmem()),
        compiler_params=pltpu.CompilerParams(vmem_limit_bytes=16 << 20),
        cost_estimate=pl.CostEstimate(flops=2 * 8 * 64 * 4096 * 128, bytes_accessed=1 << 19, transcendentals=0),
        name="row_tables",
    )(effective_rows)


def attend_kernel(base, blocks, first, last, count_ref, query_ref, mask_ref, pos_ref, *refs):
    halves, packed_ref = refs[: 2 * blocks], refs[-1]
    refs = refs[:-1]
    refs = refs[2 * blocks :]
    if not first:
        high_in, total_in, acc_in = refs[:3]
        refs = refs[3:]
    if last:
        (out_ref, high_ref, total_ref, acc_ref) = refs
    else:
        high_ref, total_ref, acc_ref = refs
    if first:
        high_ref[...] = jnp.full((QROWS, STAT), LOWEST, jnp.float32)
        total_ref[...] = jnp.zeros((QROWS, STAT), jnp.float32)
        acc_ref[...] = jnp.zeros((QROWS, LAT), jnp.float32)
    else:
        high_ref[...] = high_in[...]
        total_ref[...] = total_in[...]
        acc_ref[...] = acc_in[...]
    span = blocks * PACK
    rounds = count_ref[base, 0]
    for block in range(1, blocks):
        rounds = jnp.maximum(rounds, count_ref[base + block, 0])

    def one_round(number, carry):
        absent = []
        for block in range(blocks):
            left, right = halves[2 * block], halves[2 * block + 1]
            slot = (lax.broadcasted_iota(jnp.int32, (PACK, ROWS), 0) + number * PACK).astype(jnp.float32)
            pick = jnp.where(slot == pos_ref[base + block : base + block + 1, :], 1.0, 0.0).astype(jnp.bfloat16)
            packed = lax.dot_general(left[...], pick[:, :HALF], NT, preferred_element_type=jnp.float32)
            packed = packed + lax.dot_general(right[...], pick[:, HALF:], NT, preferred_element_type=jnp.float32)
            packed_ref[:, block * PACK : (block + 1) * PACK] = packed.astype(jnp.bfloat16)
            present = lax.dot_general(
                mask_ref[base + block].astype(jnp.bfloat16), pick, NT, preferred_element_type=jnp.float32
            )
            absent.append(jnp.where(present > 0.5, 0.0, -jnp.inf))
        absent = jnp.concatenate(absent, axis=1)
        for part in range(QROWS // QTILE):
            here = slice(part * QTILE, (part + 1) * QTILE)
            scores = jnp.dot(query_ref[here, :], packed_ref[...], preferred_element_type=jnp.float32)
            scores = scores.reshape(QTILE // 64, PAIRS, HEADS, span) * SCORE_SCALE + absent[None, :, None, :]
            scores = scores.reshape(QTILE, span)
            former = high_ref[here, :1]
            newer = jnp.maximum(former, jnp.max(scores, axis=1, keepdims=True))
            weights = jnp.exp2(scores - newer)
            decay = jnp.exp2(former - newer)
            total = total_ref[here, :1] * decay + jnp.sum(weights, axis=1, keepdims=True)
            added = lax.dot_general(
                weights.astype(jnp.bfloat16), packed_ref[:LAT, :], NT, preferred_element_type=jnp.float32
            )
            acc_ref[here, :] = acc_ref[here, :] * decay + added
            high_ref[here, :] = jnp.broadcast_to(newer, (QTILE, STAT))
            total_ref[here, :] = jnp.broadcast_to(total, (QTILE, STAT))
        return carry

    lax.fori_loop(0, (rounds + (PACK - 1)) // PACK, one_round, 0)
    if last:
        out_ref[:, :LAT] = acc_ref[...].astype(jnp.bfloat16)
        lane = lax.broadcasted_iota(jnp.int32, (QROWS, STAT), 1)
        stats = split_three(high_ref[...], lane, 0) + split_three(total_ref[...], lane, 3)
        out_ref[:, LAT:] = stats.astype(jnp.bfloat16)


def attend(base, counts, query_rows, masks, positions, halves, state=None, last=False):
    blocks = len(halves) // 2
    first = state is None
    state_shapes = (
        jax.ShapeDtypeStruct((QROWS, STAT), jnp.float32),
        jax.ShapeDtypeStruct((QROWS, STAT), jnp.float32),
        jax.ShapeDtypeStruct((QROWS, LAT), jnp.float32),
    )
    if last:
        out_shape = jax.ShapeDtypeStruct((QROWS, LAT + STAT), jnp.bfloat16)
        out_specs = vmem()
        scratch = [pltpu.VMEM(s.shape, s.dtype) for s in state_shapes]
    else:
        out_shape = state_shapes
        out_specs = (vmem(), vmem(), vmem())
        scratch = []
    scratch = scratch + [pltpu.VMEM((KV, blocks * PACK), jnp.bfloat16)]
    args = [counts, query_rows, masks, positions] + list(halves) + ([] if first else list(state))

    def body(*refs):
        attend_kernel(base, blocks, first, last, *refs)

    return pl.pallas_call(
        body,
        out_shape=out_shape,
        in_specs=[smem()] + [vmem()] * (len(args) - 1),
        out_specs=out_specs,
        scratch_shapes=scratch,
        compiler_params=pltpu.CompilerParams(vmem_limit_bytes=40 << 20),
        cost_estimate=pl.CostEstimate(
            flops=blocks * 2 * PACK * ROWS * (KV + KV + LAT), bytes_accessed=8 << 20, transcendentals=blocks * QROWS * PACK
        ),
        name="attend_%d" % blocks,
    )(*args)


def project_kernel(place_ref, recv_ref, value_ref, out_proj_ref, partial_ref, out_ref, weights, sems):
    depth = weights.shape[0] // PIECES
    copies = [
        pltpu.make_async_copy(
            out_proj_ref.at[pl.ds(piece * depth, depth)], weights.at[pl.ds(piece * depth, depth)], sems.at[piece]
        )
        for piece in range(PIECES)
    ]
    for copy in copies:
        copy.start()
    row = lax.broadcasted_iota(jnp.int32, (STAT, 2 * STAT), 0)
    col = lax.broadcasted_iota(jnp.int32, (STAT, 2 * STAT), 1)
    spread = jnp.where((row // 3) == (col // STAT), 1.0, 0.0).astype(jnp.bfloat16)
    stats = [
        jnp.dot(recv_ref[owner, :, LAT:], spread, preferred_element_type=jnp.float32) for owner in range(TP)
    ]
    highest = stats[0][:, :STAT]
    for owner in range(1, TP):
        highest = jnp.maximum(highest, stats[owner][:, :STAT])
    total = jnp.zeros((PAIRS * HEADS, STAT), jnp.float32)
    acc = jnp.zeros((PAIRS * HEADS, LAT), jnp.float32)
    for owner in range(TP):
        weight = jnp.exp2(stats[owner][:, :STAT] - highest)
        total = total + weight * stats[owner][:, STAT:]
        wide = jnp.concatenate([weight] * (LAT // STAT), axis=1)
        acc = acc + wide * recv_ref[owner, :, :LAT].astype(jnp.float32)
    attn = (acc / jnp.concatenate([total] * (LAT // STAT), axis=1)).astype(jnp.bfloat16)
    head_of = lax.broadcasted_iota(jnp.int32, (PAIRS, HEADS, 128), 1)
    pieces = []
    for head in range(HEADS):
        product = jnp.dot(attn, value_ref[head], preferred_element_type=jnp.float32)
        product = jnp.where(head_of == head, product.reshape(PAIRS, HEADS, 128), 0.0)
        pieces.append(jnp.sum(product, axis=1))
    values = jnp.concatenate(pieces, axis=1).astype(jnp.bfloat16)
    width = weights.shape[1]
    result = jnp.zeros((PAIRS, width), jnp.float32)
    for piece, copy in enumerate(copies):
        copy.wait()
        here = slice(piece * depth, (piece + 1) * depth)
        result = result + jnp.dot(values[:, here], weights[here, :], preferred_element_type=jnp.float32)
    out_ref[:, :width] = result.astype(jnp.bfloat16)
    lane = lax.broadcasted_iota(jnp.int32, (PAIRS, STAT), 1)
    group = place_ref[0] * 2 + place_ref[1]
    mine = jnp.sum(jnp.where(lane == group, partial_ref[...], 0.0), axis=1, keepdims=True)
    out_ref[:, width:] = split_three(mine, lane, 0).astype(jnp.bfloat16)


def project(place, received, value_proj, out_proj, partial):
    return pl.pallas_call(
        project_kernel,
        out_shape=jax.ShapeDtypeStruct((PAIRS, out_proj.shape[1] + STAT), jnp.bfloat16),
        in_specs=[smem(), vmem(), vmem(), pl.BlockSpec(memory_space=pltpu.HBM), vmem()],
        out_specs=vmem(),
        scratch_shapes=[pltpu.VMEM(out_proj.shape, out_proj.dtype), pltpu.SemaphoreType.DMA((PIECES,))],
        compiler_params=pltpu.CompilerParams(vmem_limit_bytes=60 << 20),
        cost_estimate=pl.CostEstimate(flops=2 * 8 * 1024 * 7168, bytes_accessed=18 << 20, transcendentals=0),
        name="project",
    )(place, received, value_proj, out_proj, partial)


def gather_kernel(own_ref, other_ref, unused_low, unused_high, out_ref):
    out_ref[0] = own_ref[...]
    out_ref[1] = other_ref[...]


def paired(own, other, far):
    return pl.pallas_call(
        gather_kernel,
        out_shape=jax.ShapeDtypeStruct((2,) + own.shape, own.dtype),
        in_specs=[vmem(), vmem()] + [pl.BlockSpec(memory_space=pl.ANY)] * 2,
        out_specs=vmem(),
        compiler_params=pltpu.CompilerParams(vmem_limit_bytes=4 << 20),
        cost_estimate=pl.CostEstimate(flops=1000, bytes_accessed=1 << 19, transcendentals=0),
        name="index_pair",
    )(own, other, *far)


def index_kernel(place_ref, here_ref, one_ref, two_ref, three_ref, key_ref, unused_ref, out_ref):
    keys = key_ref[...].astype(jnp.bfloat16)
    slabs = (here_ref, one_ref, two_ref, three_ref)
    gates = jnp.concatenate([ref[core, PAIRS * 64 :, :] for ref in slabs for core in range(2)], axis=0)
    gates = gates.astype(jnp.float32).T
    lane = lax.broadcasted_iota(jnp.int32, (PAIRS, 128), 1)
    result = jnp.zeros((PAIRS, 128), jnp.float32)
    for step, ref in enumerate(slabs):
        chip = (place_ref[0] + step) & 3
        for core in range(2):
            group = chip * 2 + (core ^ place_ref[1])
            scores = []
            for part in range(4):
                logits = lax.dot_general(
                    ref[core, part * 128 : (part + 1) * 128, :], keys, NT, preferred_element_type=jnp.float32
                )
                column = (step * 2 + core) * 16 + part
                gated = jnp.maximum(logits, 0.0) * gates[:, column : column + 1]
                scores.append(jnp.sum(gated.reshape(2, 64, ROWS), axis=1))
            scores = jnp.concatenate(scores, axis=0) * IDX ** (-0.5)
            largest = jnp.max(scores, axis=1, keepdims=True)
            summed = jnp.sum(jnp.exp(scores - largest), axis=1, keepdims=True)
            result = jnp.where(lane == group, largest + jnp.log(summed), result)
    out_ref[...] = result


def index_partial(place, slabs, index_keys, payload):
    return pl.pallas_call(
        index_kernel,
        out_shape=jax.ShapeDtypeStruct((PAIRS, 128), jnp.float32),
        in_specs=[smem()] + [vmem()] * 5 + [pl.BlockSpec(memory_space=pl.ANY)],
        out_specs=vmem(),
        compiler_params=pltpu.CompilerParams(vmem_limit_bytes=16 << 20),
        cost_estimate=pl.CostEstimate(flops=2 * 4096 * 1024 * 256, bytes_accessed=2 << 20, transcendentals=0),
        name="index_partial",
    )(place, *slabs, index_keys, payload)


def log_add(one, two):
    top = jnp.maximum(one, two)
    return top + jnp.log(jnp.exp(one - top) + jnp.exp(two - top))


def split_three(value, lane, start):
    pieces = jnp.zeros(lane.shape, jnp.float32)
    for step in range(3):
        piece = value.astype(jnp.bfloat16).astype(jnp.float32)
        pieces = jnp.where(lane == start + step, piece, pieces)
        value = value - piece
    return pieces


def join_three(pieces, start):
    wide = pieces.astype(jnp.float32)
    return wide[:, start : start + 1] + wide[:, start + 1 : start + 2] + wide[:, start + 2 : start + 3]


def four_sum(refs):
    width = refs[0].shape[1] - STAT
    parts = [ref[:, :width].astype(jnp.float32) for ref in refs]
    logs = [join_three(ref[:, width:], 0) for ref in refs]
    return (parts[0] + parts[1]) + (parts[2] + parts[3]), log_add(log_add(logs[0], logs[1]), log_add(logs[2], logs[3]))


def middle_kernel(own_ref, far_ref, right_ref, left_ref, out_ref):
    summed, logs = four_sum((own_ref, far_ref, right_ref, left_ref))
    width = summed.shape[1]
    out_ref[:, :width] = summed.astype(jnp.bfloat16)
    lane = lax.broadcasted_iota(jnp.int32, (PAIRS, STAT), 1)
    out_ref[:, width:] = split_three(logs, lane, 0).astype(jnp.bfloat16)


def final_kernel(own_ref, far_ref, right_ref, left_ref, out_ref, log_ref):
    summed, logs = four_sum((own_ref, far_ref, right_ref, left_ref))
    out_ref[...] = summed.astype(jnp.bfloat16)
    log_ref[...] = jnp.broadcast_to(logs, log_ref.shape)


def summed_over(value, shift, final):
    parts = (value,) + tuple(lax.ppermute(value, "tp", shift(step)) for step in (2, 1, 3))
    if final:
        out_shape = (
            jax.ShapeDtypeStruct((PAIRS, value.shape[1] - STAT), jnp.bfloat16),
            jax.ShapeDtypeStruct((PAIRS, STAT), jnp.float32),
        )
        out_specs = (vmem(), vmem())
    else:
        out_shape = jax.ShapeDtypeStruct(value.shape, jnp.bfloat16)
        out_specs = vmem()
    return pl.pallas_call(
        final_kernel if final else middle_kernel,
        out_shape=out_shape,
        in_specs=[vmem()] * 4,
        out_specs=out_specs,
        compiler_params=pltpu.CompilerParams(vmem_limit_bytes=4 << 20),
        cost_estimate=pl.CostEstimate(flops=1 << 18, bytes_accessed=1 << 19, transcendentals=0),
        name="sum_last" if final else "sum_first",
    )(*parts)


def x_shift(step):
    return [(x * 2 + c, ((x + step) % 4) * 2 + c) for x in range(4) for c in range(2)]


def y_shift(step):
    return [(z * 4 + y, z * 4 + (y + step) % 4) for z in range(4) for y in range(4)]


def z_shift(step):
    return [(z * 4 + y, ((z + step) % 4) * 4 + y) for z in range(4) for y in range(4)]


CORE_SWAP = [(i, i ^ 1) for i in range(PRE)]


def on_device(
    latent_rows,
    index_keys,
    queries,
    index_queries,
    index_gates,
    value_proj,
    out_proj,
    block_rows,
    block_owner,
    block_count,
):
    me_pre = lax.axis_index("pre")
    me_tp = lax.axis_index("tp")

    block = latent_rows.T.astype(jnp.bfloat16)
    low, high = block[:, :HALF], block[:, HALF:]
    fwd_low = lax.ppermute(low, "pre", x_shift(1))
    bwd_high = lax.ppermute(high, "pre", x_shift(3))
    fwd_high = lax.ppermute(high, "pre", x_shift(1))
    bwd_low = lax.ppermute(low, "pre", x_shift(3))

    def with_swapped(parts):
        return parts + [lax.ppermute(part, "pre", CORE_SWAP) for part in parts]

    own_queries = queries.reshape(PAIRS * HEADS, KV)
    all_queries = lax.all_to_all(
        jnp.broadcast_to(own_queries[None], (TP, PAIRS * HEADS, KV)), "tp", 0, 0
    ).reshape(QROWS, KV)

    fwd_low, bwd_high, all_queries = lax.optimization_barrier((fwd_low, bwd_high, all_queries))
    far_low = lax.ppermute(fwd_low, "pre", x_shift(1))
    far_high = lax.ppermute(bwd_high, "pre", x_shift(3))

    valid = (jnp.arange(BLOCK, dtype=jnp.int32) < block_count[..., None]) & (block_owner == me_tp)[..., None]
    source = block_rows >> 10
    relative = ((((source >> 1) - (me_pre >> 1) + 1) & 3) << 1) | ((source ^ me_pre) & 1)
    effective = jnp.where(valid, (relative << 10) | (block_rows & (ROWS - 1)), -1).reshape(PAIRS, -1)
    masks, positions, counts = make_tables(effective)

    near = with_swapped([fwd_low, fwd_high]) + with_swapped([low, high]) + with_swapped([bwd_low, bwd_high])
    state = attend(0, counts, all_queries, masks, positions, near)
    far_low, far_high, high, total, acc = lax.optimization_barrier((far_low, far_high) + tuple(state))
    state = (high, total, acc)
    far = with_swapped([far_low, far_high])
    payload = attend(6, counts, all_queries, masks, positions, far, state, last=True)
    received = lax.all_to_all(payload.reshape(TP, PAIRS * HEADS, LAT + STAT), "tp", 0, 0)

    gate_rows = jnp.pad(index_gates.reshape(4, IDX), ((0, 12), (0, 0)))
    piece = jnp.concatenate([index_queries.reshape(PAIRS * 64, IDX), gate_rows], axis=0)
    slab = paired(piece, lax.ppermute(piece, "pre", CORE_SWAP), far[:2])
    slabs = [slab] + [lax.ppermute(slab, "pre", x_shift(4 - step)) for step in (1, 2, 3)]
    place = jnp.stack([me_pre >> 1, me_pre & 1]).astype(jnp.int32)
    partial = index_partial(place, slabs, index_keys, payload)
    partial = log_add(partial, lax.ppermute(partial, "pre", CORE_SWAP))
    parts = [lax.ppermute(partial, "pre", x_shift(step)) for step in (2, 1, 3)]
    partial = log_add(log_add(partial, parts[0]), log_add(parts[1], parts[2]))
    part_out = project(place, received, value_proj, out_proj, partial)
    attended, index_total = summed_over(summed_over(part_out, y_shift, False), z_shift, True)
    index_total = index_total[:, 0]
    steps, queries_local = queries.shape[0], queries.shape[1]
    return (
        attended.reshape(steps, queries_local, out_proj.shape[1]),
        index_total.reshape(steps, queries_local),
    )


def solution(mesh):
    placed = (
        P(("pre", "tp"), None),
        P(("pre", "tp"), None),
        P(None, "pre", "tp", None),
        P(None, "pre", None, None),
        P(None, "pre", None),
        P("tp", None, None),
        P("tp", None),
        P(None, "pre", None, None),
        P(None, "pre", None),
        P(None, "pre", None),
    )
    return jax.shard_map(
        on_device,
        mesh=mesh,
        in_specs=placed,
        out_specs=(P(None, "pre", None), P(None, "pre")),
        check_vma=False,
    )
```

profile of v0, /device:TPU:0, one launch (start us, length us, event | category | flops | bytes accessed | tf_op | source)
XLA Modules:
  0.0 137.5 jit_solution(5073010289015142390)
XLA Ops:
  0.6 2.1 %broadcast_in_dim.16 = bf16[16,64,576]{2,1,0:T(8,128)(2,1)} broadcast(bf16[64,576]{1,0:T(8,128)(2,1)} %bitcast.15), dimensions={1,2} | broadcast | bytes 1253376 | tf_op jit(solution)/shard_map/broadcast_in_dim | solution.py:401
  2.8 8.1 %all-to-all-start = ((bf16[16,64,576]{2,1,0:T(8,128)(2,1)}), bf16[16,64,576]{2,1,0:T(8,128)(2,1)S(1)}, u32[]{:S(2)}, u32[]{:S(2)}) async-start(bf16[16,64,576]{2,1,0:T(8,128)(2,1)} %broadcast_in_dim.16), calls=%async_computation | async-start | bytes 2621440 | tf_op jit(solution)/shard_map/all_to_all | solution.py:400
  10.9 1.8 %convert_bitcast_fusion = bf16[576,1024]{1,0:T(8,128)(2,1)S(1)} fusion(f32[1024,576]{0,1:T(8,128)} %param.10), kind=kLoop, calls=%fused_computation | loop fusion | flops 589824 | bytes 3538944 | tf_op jit(solution)/shard_map/convert_element_type | solution.py:389
  12.9 1.6 %collective-permute-start = (bf16[576,512]{1,0:T(8,128)(2,1)S(1)}, bf16[576,512]{1,0:T(8,128)(2,1)}, u32[]{:S(2)}, u32[]{:S(2)}) collective-permute-start(bf16[576,512]{1,0:T(8,128)(2,1)S(1)} %get-tuple-element.35.refs_8_), channel_id=1, source_target_pairs={{0,32},{16,48},{32,64},{48,80},{64,96},{80,112},{96,0},{112,16},{1... | collective-permute-start | bytes 1769480 | tf_op jit(solution)/shard_map/ppermute | solution.py:391
  14.4 1.7 %collective-permute-start.9 = (bf16[576,512]{1,0:T(8,128)(2,1)S(1)}, bf16[576,512]{1,0:T(8,128)(2,1)S(1)}, u32[]{:S(2)}, u32[]{:S(2)}) collective-permute-start(bf16[576,512]{1,0:T(8,128)(2,1)S(1)} %get-tuple-element.35.refs_8_), channel_id=1, source_target_pairs={{0,96},{16,112},{32,0},{48,16},{64,32},{80,48},{96,64},{112,80},{1... | collective-permute-start | bytes 1769480 | tf_op jit(solution)/shard_map/ppermute | solution.py:394
  16.4 3.0 %collective-permute-start.1 = (bf16[576,512]{1,0:T(8,128)(2,1)S(1)}, bf16[576,512]{1,0:T(8,128)(2,1)}, u32[]{:S(2)}, u32[]{:S(2)}) collective-permute-start(bf16[576,512]{1,0:T(8,128)(2,1)S(1)} %get-tuple-element.34.refs_9_), channel_id=1, source_target_pairs={{0,96},{16,112},{32,0},{48,16},{64,32},{80,48},{96,64},{112,80},{1... | collective-permute-start | bytes 1769480 | tf_op jit(solution)/shard_map/ppermute | solution.py:392
  19.4 0.8 copy-done
  20.2 10.3 %collective-permute-done.refs_4_ = bf16[576,512]{1,0:T(8,128)(2,1)} collective-permute-done((bf16[576,512]{1,0:T(8,128)(2,1)S(1)}, bf16[576,512]{1,0:T(8,128)(2,1)}, u32[]{:S(2)}, u32[]{:S(2)}) %collective-permute-start) | collective-permute-done | bytes 589856 | tf_op jit(solution)/shard_map/ppermute | solution.py:391
  31.0 0.8 copy-done.4
  31.9 9.8 %collective-permute-done.4.refs_5_ = bf16[576,512]{1,0:T(8,128)(2,1)} collective-permute-done((bf16[576,512]{1,0:T(8,128)(2,1)S(1)}, bf16[576,512]{1,0:T(8,128)(2,1)}, u32[]{:S(2)}, u32[]{:S(2)}) %collective-permute-start.4) | collective-permute-done | bytes 589856 | tf_op jit(solution)/shard_map/ppermute | solution.py:393
  41.7 0.5 collective-permute-start.11
  42.3 1.5 %collective-permute-start.2 = (bf16[576,512]{1,0:T(8,128)(2,1)}, bf16[576,512]{1,0:T(8,128)(2,1)S(1)}, u32[]{:S(2)}, u32[]{:S(2)}) collective-permute-start(bf16[576,512]{1,0:T(8,128)(2,1)} %collective-permute-done.refs_4_), channel_id=1, source_target_pairs={{0,32},{16,48},{32,64},{48,80},{64,96},{80,112},{96,0},{112,16},{1... | collective-permute-start | bytes 1769480 | tf_op jit(solution)/shard_map/ppermute | solution.py:405
  43.8 1.8 %collective-permute-start.3 = (bf16[576,512]{1,0:T(8,128)(2,1)}, bf16[576,512]{1,0:T(8,128)(2,1)S(1)}, u32[]{:S(2)}, u32[]{:S(2)}) collective-permute-start(bf16[576,512]{1,0:T(8,128)(2,1)} %collective-permute-done.1.refs_13_), channel_id=1, source_target_pairs={{0,96},{16,112},{32,0},{48,16},{64,32},{80,48},{96,64},{112,80},{1... | collective-permute-start | bytes 1769480 | tf_op jit(solution)/shard_map/ppermute | solution.py:406
  45.6 1.1 or_select_fusion
  46.9 3.3 %row_tables.1 = (f32[8,8,1024]{2,1,0:T(8,128)S(1)}, f32[8,1024]{1,0:T(8,128)S(1)}, s32[8,128]{1,0:T(8,128)S(1)}) custom-call(s32[8,4096]{1,0:T(8,128)S(1)} %reshape.25.rows_ref), custom_call_target="tpu_custom_call" | custom-call | flops 536870912 | bytes 524288 | tf_op jit(solution)/shard_map/row_tables/pallas_call | solution.py:67
  50.3 11.7 %attend_6.1 = (f32[1024,128]{1,0:T(8,128)S(1)}, f32[1024,128]{1,0:T(8,128)S(1)}, f32[1024,512]{1,0:T(8,128)S(1)}) custom-call(s32[8,128]{1,0:T(8,128)S(1)} %get-tuple-element.18.refs_0_, bf16[1024,576]{1,0:T(8,128)(2,1)S(1)} %bitcast.12, f32[8,8,1024]{2,1,0:T(8,128)S(1)} %get-tuple-element.20.refs_2_, f32[8,1024]{1,0:T(8,128)S(1)} %get-tuple-element.21.refs_3_, ...), custom_call_target="tpu_custom_call" | custom-call | flops 5234491392 | bytes 8388608 | tf_op jit(solution)/shard_map/attend_6/pallas_call | solution.py:168
  62.6 1.5 %collective-permute-done.12.refs_6_ = bf16[576,512]{1,0:T(8,128)(2,1)S(1)} collective-permute-done((bf16[576,512]{1,0:T(8,128)(2,1)S(1)}, bf16[576,512]{1,0:T(8,128)(2,1)S(1)}, u32[]{:S(2)}, u32[]{:S(2)}) %collective-permute-start.12) | collective-permute-done | bytes 589856 | tf_op jit(solution)/shard_map/ppermute | solution.py:397
  64.1 0.8 collective-permute-done.13.refs_7_
  64.9 6.1 %attend_2.1.unused_ref = bf16[1024,640]{1,0:T(8,128)(2,1)} custom-call(s32[8,128]{1,0:T(8,128)S(1)} %get-tuple-element.18.refs_0_, bf16[1024,576]{1,0:T(8,128)(2,1)S(1)} %bitcast.13, f32[8,8,1024]{2,1,0:T(8,128)S(1)} %get-tuple-element.20.refs_2_, f32[8,1024]{1,0:T(8,128)S(1)} %get-tuple-element.21.refs_3_, ...), custom_call_target="tpu_custom_call" | custom-call | flops 1744830464 | bytes 8388608 | tf_op jit(solution)/shard_map/attend_2/pallas_call | solution.py:168
  71.0 7.1 %all-to-all-start.1 = ((bf16[16,64,640]{2,1,0:T(8,128)(2,1)}), bf16[16,64,640]{2,1,0:T(8,128)(2,1)}, u32[]{:S(2)}, u32[]{:S(2)}) async-start(bf16[16,64,640]{2,1,0:T(8,128)(2,1)} %bitcast.5), calls=%async_computation.1 | async-start | bytes 2621440 | tf_op jit(solution)/shard_map/all_to_all | solution.py:420
  78.3 1.3 collective-permute-done.14.other_ref
  79.7 1.9 %collective-permute-start.15 = (bf16[2,528,128]{2,1,0:T(8,128)(2,1)S(1)}, bf16[2,528,128]{2,1,0:T(8,128)(2,1)S(1)}, u32[]{:S(2)}, u32[]{:S(2)}) collective-permute-start(bf16[2,528,128]{2,1,0:T(8,128)(2,1)S(1)} %index_pair.1.here_ref), channel_id=1, source_target_pairs={{0,96},{16,112},{32,0},{48,16},{64,32},{80,48},{96,64},{112,80},{1... | collective-permute-start | bytes 811016 | tf_op jit(solution)/shard_map/ppermute | solution.py:425
  81.6 0.6 collective-permute-start.16
  82.2 0.6 collective-permute-start.17
  82.9 6.4 %collective-permute-done.15.one_ref = bf16[2,528,128]{2,1,0:T(8,128)(2,1)S(1)} collective-permute-done((bf16[2,528,128]{2,1,0:T(8,128)(2,1)S(1)}, bf16[2,528,128]{2,1,0:T(8,128)(2,1)S(1)}, u32[]{:S(2)}, u32[]{:S(2)}) %collective-permute-start.15) | collective-permute-done | bytes 270368 | tf_op jit(solution)/shard_map/ppermute | solution.py:425
  89.3 3.2 %collective-permute-done.16.two_ref = bf16[2,528,128]{2,1,0:T(8,128)(2,1)S(1)} collective-permute-done((bf16[2,528,128]{2,1,0:T(8,128)(2,1)S(1)}, bf16[2,528,128]{2,1,0:T(8,128)(2,1)S(1)}, u32[]{:S(2)}, u32[]{:S(2)}) %collective-permute-start.16) | collective-permute-done | bytes 270368 | tf_op jit(solution)/shard_map/ppermute | solution.py:425
  92.6 4.6 %collective-permute-done.17.three_ref = bf16[2,528,128]{2,1,0:T(8,128)(2,1)S(1)} collective-permute-done((bf16[2,528,128]{2,1,0:T(8,128)(2,1)S(1)}, bf16[2,528,128]{2,1,0:T(8,128)(2,1)S(1)}, u32[]{:S(2)}, u32[]{:S(2)}) %collective-permute-start.17) | collective-permute-done | bytes 270368 | tf_op jit(solution)/shard_map/ppermute | solution.py:425
  97.2 3.2 %index_partial.1 = f32[8,128]{1,0:T(8,128)S(1)} custom-call(s32[2]{0:T(128)S(1)} %pad_add_fusion.place_ref, bf16[2,528,128]{2,1,0:T(8,128)(2,1)S(1)} %index_pair.1.here_ref, bf16[2,528,128]{2,1,0:T(8,128)(2,1)S(1)} %collective-permute-done.15.one_ref, bf16[2,528,128]{2,1,0:T(8,128)(2,1)S(1)} %collective-permute-done.16.two_ref, ...), custom_call_target="tpu_custom_call" | custom-call | flops 2147483648 | bytes 2097152 | tf_op jit(solution)/shard_map/index_partial/pallas_call | solution.py:286
  100.5 1.1 collective-permute-done.18
  101.6 0.7 collective-permute-start.19
  102.3 0.9 collective-permute-start.20
  103.2 2.4 %collective-permute-start.21 = (f32[8,128]{1,0:T(8,128)S(1)}, f32[8,128]{1,0:T(8,128)S(1)}, u32[]{:S(2)}, u32[]{:S(2)}) collective-permute-start(f32[8,128]{1,0:T(8,128)S(1)} %log_add_fusion.1), channel_id=1, source_target_pairs={{0,96},{16,112},{32,0},{48,16},{64,32},{80,48},{96,64},{112,80},{1... | collective-permute-start | bytes 12296 | tf_op jit(solution)/shard_map/ppermute | solution.py:429
  105.5 1.3 collective-permute-done.19
  107.1 0.6 log_add_fusion.partial_ref
  107.8 8.2 %project.1.own_ref = bf16[8,7296]{1,0:T(8,128)(2,1)} custom-call(s32[2]{0:T(128)} %copy-done.3, bf16[16,64,640]{2,1,0:T(8,128)(2,1)} %all-to-all-done.1.recv_ref, bf16[8,512,128]{2,1,0:T(8,128)(2,1)} %value_ref.1, bf16[1024,7168]{1,0:T(8,128)(2,1)} %out_proj_ref.1, f32[8,128]{1,0:T(8,128)} %log_add_fusion.partial_ref), custom_call_target="tpu_custom_call" | custom-call | flops 117440512 | bytes 18874368 | tf_op jit(solution)/shard_map/project/pallas_call | solution.py:230
  115.9 3.5 %collective-permute-start.22 = (bf16[8,7296]{1,0:T(8,128)(2,1)}, bf16[8,7296]{1,0:T(8,128)(2,1)S(1)}, u32[]{:S(2)}, u32[]{:S(2)}) collective-permute-start(bf16[8,7296]{1,0:T(8,128)(2,1)} %project.1.own_ref), channel_id=1, source_target_pairs={{0,2},{1,3},{2,0},{3,1},{4,6},{5,7},{6,4},{7,5},{8,10},{9,11},{10,... | collective-permute-start | bytes 350216 | tf_op jit(solution)/shard_map/ppermute | solution.py:338
  119.4 0.6 collective-permute-start.23
  120.0 2.7 %collective-permute-start.24 = (bf16[8,7296]{1,0:T(8,128)(2,1)}, bf16[8,7296]{1,0:T(8,128)(2,1)S(1)}, u32[]{:S(2)}, u32[]{:S(2)}) collective-permute-start(bf16[8,7296]{1,0:T(8,128)(2,1)} %project.1.own_ref), channel_id=1, source_target_pairs={{0,3},{1,0},{2,1},{3,2},{4,7},{5,4},{6,5},{7,6},{8,11},{9,8},{10,9... | collective-permute-start | bytes 350216 | tf_op jit(solution)/shard_map/ppermute | solution.py:338
  122.6 1.2 collective-permute-done.22.far_ref
  123.9 1.8 %collective-permute-done.23.right_ref = bf16[8,7296]{1,0:T(8,128)(2,1)S(1)} collective-permute-done((bf16[8,7296]{1,0:T(8,128)(2,1)}, bf16[8,7296]{1,0:T(8,128)(2,1)S(1)}, u32[]{:S(2)}, u32[]{:S(2)}) %collective-permute-start.23) | collective-permute-done | bytes 116768 | tf_op jit(solution)/shard_map/ppermute | solution.py:338
  125.6 0.9 copy-done.2
  126.8 3.0 %collective-permute-start.25 = (bf16[8,7296]{1,0:T(8,128)(2,1)S(1)}, bf16[8,7296]{1,0:T(8,128)(2,1)S(1)}, u32[]{:S(2)}, u32[]{:S(2)}) collective-permute-start(bf16[8,7296]{1,0:T(8,128)(2,1)S(1)} %sum_first.1.own_ref), channel_id=1, source_target_pairs={{0,8},{1,9},{2,10},{3,11},{4,12},{5,13},{6,14},{7,15},{8,0},{9,1},... | collective-permute-start | bytes 350216 | tf_op jit(solution)/shard_map/ppermute | solution.py:338
  129.8 0.6 collective-permute-start.26
  130.4 2.7 %collective-permute-start.27 = (bf16[8,7296]{1,0:T(8,128)(2,1)S(1)}, bf16[8,7296]{1,0:T(8,128)(2,1)S(1)}, u32[]{:S(2)}, u32[]{:S(2)}) collective-permute-start(bf16[8,7296]{1,0:T(8,128)(2,1)S(1)} %sum_first.1.own_ref), channel_id=1, source_target_pairs={{0,12},{1,13},{2,14},{3,15},{4,0},{5,1},{6,2},{7,3},{8,4},{9,5},{1... | collective-permute-start | bytes 350216 | tf_op jit(solution)/shard_map/ppermute | solution.py:338
  133.0 0.7 collective-permute-done.25.far_ref
  133.7 2.1 %collective-permute-done.26.right_ref = bf16[8,7296]{1,0:T(8,128)(2,1)S(1)} collective-permute-done((bf16[8,7296]{1,0:T(8,128)(2,1)S(1)}, bf16[8,7296]{1,0:T(8,128)(2,1)S(1)}, u32[]{:S(2)}, u32[]{:S(2)}) %collective-permute-start.26) | collective-permute-done | bytes 116768 | tf_op jit(solution)/shard_map/ppermute | solution.py:338
  136.1 0.7 reshape.30
  136.9 0.6 reshape_squeeze.3
  (56 shorter events, 3.0 us)
Async XLA Ops:
  2.8 38.9 %all-to-all-start = ((bf16[16,64,576]{2,1,0:T(8,128)(2,1)}), bf16[16,64,576]{2,1,0:T(8,128)(2,1)S(1)}, u32[]{:S(2)}, u32[]{:S(2)}) async-start(bf16[16,64,576]{2,1,0:T(8,128)(2,1)} %broadcast_in_dim.16), calls=%async_computation | async-start | bytes 2621440 | tf_op jit(solution)/shard_map/all_to_all | solution.py:400
  12.8 29.5 %copy-start.9 = (s32[2,4,64]{2,1,0:T(4,128)S(1)}, s32[2,4,64]{2,1,0:T(4,128)}, u32[]{:S(2)}) copy-start(s32[2,4,64]{2,1,0:T(4,128)} %param.18) | copy-start | bytes 6148
  12.8 32.9 %copy-start.8 = (s32[2,4,64]{2,1,0:T(4,128)S(1)}, s32[2,4,64]{2,1,0:T(4,128)}, u32[]{:S(2)}) copy-start(s32[2,4,64]{2,1,0:T(4,128)} %param.19) | copy-start | bytes 6148
  12.9 17.6 %collective-permute-start = (bf16[576,512]{1,0:T(8,128)(2,1)S(1)}, bf16[576,512]{1,0:T(8,128)(2,1)}, u32[]{:S(2)}, u32[]{:S(2)}) collective-permute-start(bf16[576,512]{1,0:T(8,128)(2,1)S(1)} %get-tuple-element.35.refs_8_), channel_id=1, source_target_pairs={{0,32},{16,48},{32,64},{48,80},{64,96},{80,112},{96,0},{112,16},{1... | collective-permute-start | bytes 1769480 | tf_op jit(solution)/shard_map/ppermute | solution.py:391
  14.4 16.3 %collective-permute-start.9 = (bf16[576,512]{1,0:T(8,128)(2,1)S(1)}, bf16[576,512]{1,0:T(8,128)(2,1)S(1)}, u32[]{:S(2)}, u32[]{:S(2)}) collective-permute-start(bf16[576,512]{1,0:T(8,128)(2,1)S(1)} %get-tuple-element.35.refs_8_), channel_id=1, source_target_pairs={{0,96},{16,112},{32,0},{48,16},{64,32},{80,48},{96,64},{112,80},{1... | collective-permute-start | bytes 1769480 | tf_op jit(solution)/shard_map/ppermute | solution.py:394
  16.2 25.5 %collective-permute-start.4 = (bf16[576,512]{1,0:T(8,128)(2,1)S(1)}, bf16[576,512]{1,0:T(8,128)(2,1)}, u32[]{:S(2)}, u32[]{:S(2)}) collective-permute-start(bf16[576,512]{1,0:T(8,128)(2,1)S(1)} %get-tuple-element.34.refs_9_), channel_id=1, source_target_pairs={{0,32},{16,48},{32,64},{48,80},{64,96},{80,112},{96,0},{112,16},{1... | collective-permute-start | bytes 1769480 | tf_op jit(solution)/shard_map/ppermute | solution.py:393
  16.4 25.2 %collective-permute-start.1 = (bf16[576,512]{1,0:T(8,128)(2,1)S(1)}, bf16[576,512]{1,0:T(8,128)(2,1)}, u32[]{:S(2)}, u32[]{:S(2)}) collective-permute-start(bf16[576,512]{1,0:T(8,128)(2,1)S(1)} %get-tuple-element.34.refs_9_), channel_id=1, source_target_pairs={{0,96},{16,112},{32,0},{48,16},{64,32},{80,48},{96,64},{112,80},{1... | collective-permute-start | bytes 1769480 | tf_op jit(solution)/shard_map/ppermute | solution.py:392
  19.4 22.8 %collective-permute-start.7 = (bf16[576,512]{1,0:T(8,128)(2,1)S(1)}, bf16[576,512]{1,0:T(8,128)(2,1)}, u32[]{:S(2)}, u32[]{:S(2)}) collective-permute-start(bf16[576,512]{1,0:T(8,128)(2,1)S(1)} %get-tuple-element.35.refs_8_), channel_id=1, source_target_pairs={{0,16},{16,0},{32,48},{48,32},{64,80},{80,64},{96,112},{112,96},{1... | collective-permute-start | bytes 1769480 | tf_op jit(solution)/shard_map/ppermute | solution.py:397
  19.4 0.8 copy-start
  30.5 11.8 %collective-permute-start.8 = (bf16[576,512]{1,0:T(8,128)(2,1)S(1)}, bf16[576,512]{1,0:T(8,128)(2,1)}, u32[]{:S(2)}, u32[]{:S(2)}) collective-permute-start(bf16[576,512]{1,0:T(8,128)(2,1)S(1)} %get-tuple-element.34.refs_9_), channel_id=1, source_target_pairs={{0,16},{16,0},{32,48},{48,32},{64,80},{80,64},{96,112},{112,96},{1... | collective-permute-start | bytes 1769480 | tf_op jit(solution)/shard_map/ppermute | solution.py:397
  30.7 13.1 %collective-permute-start.10 = (bf16[576,512]{1,0:T(8,128)(2,1)S(1)}, bf16[576,512]{1,0:T(8,128)(2,1)}, u32[]{:S(2)}, u32[]{:S(2)}) collective-permute-start(bf16[576,512]{1,0:T(8,128)(2,1)S(1)} %collective-permute-done.9.refs_12_), channel_id=1, source_target_pairs={{0,16},{16,0},{32,48},{48,32},{64,80},{80,64},{96,112},{112,96},{1... | collective-permute-start | bytes 1769480 | tf_op jit(solution)/shard_map/ppermute | solution.py:397
  31.0 0.8 copy-start.4
  41.7 8.5 %collective-permute-start.6 = (bf16[576,512]{1,0:T(8,128)(2,1)}, bf16[576,512]{1,0:T(8,128)(2,1)}, u32[]{:S(2)}, u32[]{:S(2)}) collective-permute-start(bf16[576,512]{1,0:T(8,128)(2,1)} %collective-permute-done.4.refs_5_), channel_id=1, source_target_pairs={{0,16},{16,0},{32,48},{48,32},{64,80},{80,64},{96,112},{112,96},{1... | collective-permute-start | bytes 1769480 | tf_op jit(solution)/shard_map/ppermute | solution.py:397
  41.7 8.5 %collective-permute-start.11 = (bf16[576,512]{1,0:T(8,128)(2,1)}, bf16[576,512]{1,0:T(8,128)(2,1)}, u32[]{:S(2)}, u32[]{:S(2)}) collective-permute-start(bf16[576,512]{1,0:T(8,128)(2,1)} %collective-permute-done.1.refs_13_), channel_id=1, source_target_pairs={{0,16},{16,0},{32,48},{48,32},{64,80},{80,64},{96,112},{112,96},{1... | collective-permute-start | bytes 1769480 | tf_op jit(solution)/shard_map/ppermute | solution.py:397
  42.2 8.0 %collective-permute-start.5 = (bf16[576,512]{1,0:T(8,128)(2,1)}, bf16[576,512]{1,0:T(8,128)(2,1)}, u32[]{:S(2)}, u32[]{:S(2)}) collective-permute-start(bf16[576,512]{1,0:T(8,128)(2,1)} %collective-permute-done.refs_4_), channel_id=1, source_target_pairs={{0,16},{16,0},{32,48},{48,32},{64,80},{80,64},{96,112},{112,96},{1... | collective-permute-start | bytes 1769480 | tf_op jit(solution)/shard_map/ppermute | solution.py:397
  42.3 19.7 %collective-permute-start.2 = (bf16[576,512]{1,0:T(8,128)(2,1)}, bf16[576,512]{1,0:T(8,128)(2,1)S(1)}, u32[]{:S(2)}, u32[]{:S(2)}) collective-permute-start(bf16[576,512]{1,0:T(8,128)(2,1)} %collective-permute-done.refs_4_), channel_id=1, source_target_pairs={{0,32},{16,48},{32,64},{48,80},{64,96},{80,112},{96,0},{112,16},{1... | collective-permute-start | bytes 1769480 | tf_op jit(solution)/shard_map/ppermute | solution.py:405
  43.8 18.2 %collective-permute-start.3 = (bf16[576,512]{1,0:T(8,128)(2,1)}, bf16[576,512]{1,0:T(8,128)(2,1)S(1)}, u32[]{:S(2)}, u32[]{:S(2)}) collective-permute-start(bf16[576,512]{1,0:T(8,128)(2,1)} %collective-permute-done.1.refs_13_), channel_id=1, source_target_pairs={{0,96},{16,112},{32,0},{48,16},{64,32},{80,48},{96,64},{112,80},{1... | collective-permute-start | bytes 1769480 | tf_op jit(solution)/shard_map/ppermute | solution.py:406
  46.9 3.3 %copy-start.1 = (bf16[576,512]{1,0:T(8,128)(2,1)S(1)}, bf16[576,512]{1,0:T(8,128)(2,1)}, u32[]{:S(2)}) copy-start(bf16[576,512]{1,0:T(8,128)(2,1)} %copy-done) | copy-start | bytes 1769476
  46.9 3.4 %copy-start.5 = (bf16[576,512]{1,0:T(8,128)(2,1)S(1)}, bf16[576,512]{1,0:T(8,128)(2,1)}, u32[]{:S(2)}) copy-start(bf16[576,512]{1,0:T(8,128)(2,1)} %copy-done.4) | copy-start | bytes 1769476
  62.0 2.1 %collective-permute-start.12 = (bf16[576,512]{1,0:T(8,128)(2,1)S(1)}, bf16[576,512]{1,0:T(8,128)(2,1)S(1)}, u32[]{:S(2)}, u32[]{:S(2)}) collective-permute-start(bf16[576,512]{1,0:T(8,128)(2,1)S(1)} %collective-permute-done.2.refs_4_.unused_low), channel_id=1, source_target_pairs={{0,16},{16,0},{32,48},{48,32},{64,80},{80,64},{96,112},{112,96},{1... | collective-permute-start | bytes 1769480 | tf_op jit(solution)/shard_map/ppermute | solution.py:397
  62.1 2.8 %collective-permute-start.13 = (bf16[576,512]{1,0:T(8,128)(2,1)S(1)}, bf16[576,512]{1,0:T(8,128)(2,1)S(1)}, u32[]{:S(2)}, u32[]{:S(2)}) collective-permute-start(bf16[576,512]{1,0:T(8,128)(2,1)S(1)} %collective-permute-done.3.refs_5_.unused_high), channel_id=1, source_target_pairs={{0,16},{16,0},{32,48},{48,32},{64,80},{80,64},{96,112},{112,96},{1... | collective-permute-start | bytes 1769480 | tf_op jit(solution)/shard_map/ppermute | solution.py:397
  71.0 7.1 %copy-start.10 = (bf16[2,4,64]{2,1,0:T(4,128)(2,1)S(1)}, bf16[2,4,64]{2,1,0:T(4,128)(2,1)}, u32[]{:S(2)}) copy-start(bf16[2,4,64]{2,1,0:T(4,128)(2,1)} %param.14) | copy-start | bytes 3076
  71.0 7.2 %copy-start.7 = (bf16[2,4,64,128]{3,2,1,0:T(8,128)(2,1)S(1)}, bf16[2,4,64,128]{3,2,1,0:T(8,128)(2,1)}, u32[]{:S(2)}) copy-start(bf16[2,4,64,128]{3,2,1,0:T(8,128)(2,1)} %param.13) | copy-start | bytes 393220
  71.0 36.8 %all-to-all-start.1 = ((bf16[16,64,640]{2,1,0:T(8,128)(2,1)}), bf16[16,64,640]{2,1,0:T(8,128)(2,1)}, u32[]{:S(2)}, u32[]{:S(2)}) async-start(bf16[16,64,640]{2,1,0:T(8,128)(2,1)} %bitcast.5), calls=%async_computation.1 | async-start | bytes 2621440 | tf_op jit(solution)/shard_map/all_to_all | solution.py:420
  78.1 19.1 %copy-start.6 = (f32[1024,128]{1,0:T(8,128)S(1)}, f32[1024,128]{1,0:T(8,128)}, u32[]{:S(2)}) copy-start(f32[1024,128]{1,0:T(8,128)} %key_ref.1) | copy-start | bytes 1572868
  78.2 1.4 %collective-permute-start.14 = (bf16[528,128]{1,0:T(8,128)(2,1)S(1)}, bf16[528,128]{1,0:T(8,128)(2,1)S(1)}, u32[]{:S(2)}, u32[]{:S(2)}) collective-permute-start(bf16[528,128]{1,0:T(8,128)(2,1)S(1)} %fusion.2.own_ref), channel_id=1, source_target_pairs={{0,16},{16,0},{32,48},{48,32},{64,80},{80,64},{96,112},{112,96},{1... | collective-permute-start | bytes 405512 | tf_op jit(solution)/shard_map/ppermute | solution.py:424
  79.7 9.6 %collective-permute-start.15 = (bf16[2,528,128]{2,1,0:T(8,128)(2,1)S(1)}, bf16[2,528,128]{2,1,0:T(8,128)(2,1)S(1)}, u32[]{:S(2)}, u32[]{:S(2)}) collective-permute-start(bf16[2,528,128]{2,1,0:T(8,128)(2,1)S(1)} %index_pair.1.here_ref), channel_id=1, source_target_pairs={{0,96},{16,112},{32,0},{48,16},{64,32},{80,48},{96,64},{112,80},{1... | collective-permute-start | bytes 811016 | tf_op jit(solution)/shard_map/ppermute | solution.py:425
  81.6 10.9 %collective-permute-start.16 = (bf16[2,528,128]{2,1,0:T(8,128)(2,1)S(1)}, bf16[2,528,128]{2,1,0:T(8,128)(2,1)S(1)}, u32[]{:S(2)}, u32[]{:S(2)}) collective-permute-start(bf16[2,528,128]{2,1,0:T(8,128)(2,1)S(1)} %index_pair.1.here_ref), channel_id=1, source_target_pairs={{0,64},{16,80},{32,96},{48,112},{64,0},{80,16},{96,32},{112,48},{1... | collective-permute-start | bytes 811016 | tf_op jit(solution)/shard_map/ppermute | solution.py:425
  82.2 14.9 %collective-permute-start.17 = (bf16[2,528,128]{2,1,0:T(8,128)(2,1)S(1)}, bf16[2,528,128]{2,1,0:T(8,128)(2,1)S(1)}, u32[]{:S(2)}, u32[]{:S(2)}) collective-permute-start(bf16[2,528,128]{2,1,0:T(8,128)(2,1)S(1)} %index_pair.1.here_ref), channel_id=1, source_target_pairs={{0,32},{16,48},{32,64},{48,80},{64,96},{80,112},{96,0},{112,16},{1... | collective-permute-start | bytes 811016 | tf_op jit(solution)/shard_map/ppermute | solution.py:425
  82.9 17.5 %copy-start.3 = (s32[2]{0:T(128)}, s32[2]{0:T(128)S(1)}, u32[]{:S(2)}) copy-start(s32[2]{0:T(128)S(1)} %pad_add_fusion.place_ref) | copy-start | bytes 28
  100.4 1.2 collective-permute-start.18
  101.6 5.2 %collective-permute-start.19 = (f32[8,128]{1,0:T(8,128)S(1)}, f32[8,128]{1,0:T(8,128)S(1)}, u32[]{:S(2)}, u32[]{:S(2)}) collective-permute-start(f32[8,128]{1,0:T(8,128)S(1)} %log_add_fusion.1), channel_id=1, source_target_pairs={{0,64},{16,80},{32,96},{48,112},{64,0},{80,16},{96,32},{112,48},{1... | collective-permute-start | bytes 12296 | tf_op jit(solution)/shard_map/ppermute | solution.py:429
  102.3 4.8 %collective-permute-start.20 = (f32[8,128]{1,0:T(8,128)S(1)}, f32[8,128]{1,0:T(8,128)S(1)}, u32[]{:S(2)}, u32[]{:S(2)}) collective-permute-start(f32[8,128]{1,0:T(8,128)S(1)} %log_add_fusion.1), channel_id=1, source_target_pairs={{0,32},{16,48},{32,64},{48,80},{64,96},{80,112},{96,0},{112,16},{1... | collective-permute-start | bytes 12296 | tf_op jit(solution)/shard_map/ppermute | solution.py:429
  103.2 4.0 %collective-permute-start.21 = (f32[8,128]{1,0:T(8,128)S(1)}, f32[8,128]{1,0:T(8,128)S(1)}, u32[]{:S(2)}, u32[]{:S(2)}) collective-permute-start(f32[8,128]{1,0:T(8,128)S(1)} %log_add_fusion.1), channel_id=1, source_target_pairs={{0,96},{16,112},{32,0},{48,16},{64,32},{80,48},{96,64},{112,80},{1... | collective-permute-start | bytes 12296 | tf_op jit(solution)/shard_map/ppermute | solution.py:429
  115.9 7.9 %collective-permute-start.22 = (bf16[8,7296]{1,0:T(8,128)(2,1)}, bf16[8,7296]{1,0:T(8,128)(2,1)S(1)}, u32[]{:S(2)}, u32[]{:S(2)}) collective-permute-start(bf16[8,7296]{1,0:T(8,128)(2,1)} %project.1.own_ref), channel_id=1, source_target_pairs={{0,2},{1,3},{2,0},{3,1},{4,6},{5,7},{6,4},{7,5},{8,10},{9,11},{10,... | collective-permute-start | bytes 350216 | tf_op jit(solution)/shard_map/ppermute | solution.py:338
  119.4 6.2 %collective-permute-start.23 = (bf16[8,7296]{1,0:T(8,128)(2,1)}, bf16[8,7296]{1,0:T(8,128)(2,1)S(1)}, u32[]{:S(2)}, u32[]{:S(2)}) collective-permute-start(bf16[8,7296]{1,0:T(8,128)(2,1)} %project.1.own_ref), channel_id=1, source_target_pairs={{0,1},{1,2},{2,3},{3,0},{4,5},{5,6},{6,7},{7,4},{8,9},{9,10},{10,1... | collective-permute-start | bytes 350216 | tf_op jit(solution)/shard_map/ppermute | solution.py:338
  120.0 5.7 %collective-permute-start.24 = (bf16[8,7296]{1,0:T(8,128)(2,1)}, bf16[8,7296]{1,0:T(8,128)(2,1)S(1)}, u32[]{:S(2)}, u32[]{:S(2)}) collective-permute-start(bf16[8,7296]{1,0:T(8,128)(2,1)} %project.1.own_ref), channel_id=1, source_target_pairs={{0,3},{1,0},{2,1},{3,2},{4,7},{5,4},{6,5},{7,6},{8,11},{9,8},{10,9... | collective-permute-start | bytes 350216 | tf_op jit(solution)/shard_map/ppermute | solution.py:338
  125.6 0.9 copy-start.2
  126.8 6.9 %collective-permute-start.25 = (bf16[8,7296]{1,0:T(8,128)(2,1)S(1)}, bf16[8,7296]{1,0:T(8,128)(2,1)S(1)}, u32[]{:S(2)}, u32[]{:S(2)}) collective-permute-start(bf16[8,7296]{1,0:T(8,128)(2,1)S(1)} %sum_first.1.own_ref), channel_id=1, source_target_pairs={{0,8},{1,9},{2,10},{3,11},{4,12},{5,13},{6,14},{7,15},{8,0},{9,1},... | collective-permute-start | bytes 350216 | tf_op jit(solution)/shard_map/ppermute | solution.py:338
  129.8 6.0 %collective-permute-start.26 = (bf16[8,7296]{1,0:T(8,128)(2,1)S(1)}, bf16[8,7296]{1,0:T(8,128)(2,1)S(1)}, u32[]{:S(2)}, u32[]{:S(2)}) collective-permute-start(bf16[8,7296]{1,0:T(8,128)(2,1)S(1)} %sum_first.1.own_ref), channel_id=1, source_target_pairs={{0,4},{1,5},{2,6},{3,7},{4,8},{5,9},{6,10},{7,11},{8,12},{9,13},{1... | collective-permute-start | bytes 350216 | tf_op jit(solution)/shard_map/ppermute | solution.py:338
  130.4 5.5 %collective-permute-start.27 = (bf16[8,7296]{1,0:T(8,128)(2,1)S(1)}, bf16[8,7296]{1,0:T(8,128)(2,1)S(1)}, u32[]{:S(2)}, u32[]{:S(2)}) collective-permute-start(bf16[8,7296]{1,0:T(8,128)(2,1)S(1)} %sum_first.1.own_ref), channel_id=1, source_target_pairs={{0,12},{1,13},{2,14},{3,15},{4,0},{5,1},{6,2},{7,3},{8,4},{9,5},{1... | collective-permute-start | bytes 350216 | tf_op jit(solution)/shard_map/ppermute | solution.py:338
where the time goes:
time: 139 us; the launch traced here: 138 us
  waiting for transfers between devices  46.8 us (34%)
  starting transfers between devices  46.7 us (34%)
  Pallas kernels  32.9 us (24%)
  local copies, waits for them, and re-layouts  6.5 us (5%)
  other arithmetic  3.72 us (3%)
    pallas_call x2, Pallas kernels, attend(): pl.pallas_call(body, out_shape=out_shape, in_specs=[smem()] + [vmem()] *...  17.8 us
    ppermute x3, waiting for transfers between devices, on_device(): lax.ppermute(slab, 'pre', x_shift(4 - step))  14.3 us
    ppermute x6, starting transfers between devices, summed_over(): lax.ppermute(value, 'tp', shift(step))  13 us
    ppermute x1, waiting for transfers between devices, on_device(): fwd_low = lax.ppermute(low, 'pre', x_shift(1))  10.3 us
    ppermute x1, waiting for transfers between devices, on_device(): fwd_high = lax.ppermute(high, 'pre', x_shift(1))  9.82 us
    pallas_call x1, Pallas kernels, project(): pl.pallas_call(project_kernel, out_shape=jax.ShapeDtypeStruct((PAIRS, out...  8.16 us
    all_to_all x1, starting transfers between devices, on_device(): lax.all_to_all(jnp.broadcast_to(own_queries[None], (TP, PAIRS * HEADS, KV...  8.13 us
    all_to_all x1, starting transfers between devices, on_device(): lax.all_to_all(payload.reshape(TP, PAIRS * HEADS, LAT + STAT), 'tp', 0, 0)  7.11 us
  transfers between devices with their start and end apart: 30, of which 16 were waited for; matrix products, arithmetic and copies ran while one was open for 3% of the time, Pallas kernels for 13%

commit v1 on v0

--- a/solution.py
+++ b/solution.py
@@ -14,7 +14,6 @@
 PAIRS = 8
 HEADS = 8
 ROWS = 1024
-HALF = 512
 PACK = 256
 QTILE = 256
 PIECES = 4
@@ -79,75 +78,85 @@
     )(effective_rows)
 
 
-def attend_kernel(base, blocks, first, last, count_ref, query_ref, mask_ref, pos_ref, *refs):
-    halves, packed_ref = refs[: 2 * blocks], refs[-1]
-    refs = refs[:-1]
-    refs = refs[2 * blocks :]
+def attend_kernel(base, parts, first, last, count_ref, query_ref, mask_ref, pos_ref, *refs):
+    blocks = len(parts)
+    sources = []
+    for number in parts:
+        sources.append(refs[:number])
+        refs = refs[number:]
     if not first:
-        high_in, total_in, acc_in = refs[:3]
+        stat_in, acc_in = refs[:2]
+        refs = refs[2:]
+    if last:
+        out_ref, stat_ref, acc_ref = refs[:3]
         refs = refs[3:]
-    if last:
-        (out_ref, high_ref, total_ref, acc_ref) = refs
     else:
-        high_ref, total_ref, acc_ref = refs
+        stat_ref, acc_ref = refs[:2]
+        refs = refs[2:]
+    (packed_ref,) = refs
     if first:
-        high_ref[...] = jnp.full((QROWS, STAT), LOWEST, jnp.float32)
-        total_ref[...] = jnp.zeros((QROWS, STAT), jnp.float32)
+        column = lax.broadcasted_iota(jnp.int32, (QROWS, STAT), 1)
+        stat_ref[...] = jnp.where(column < STAT // 2, LOWEST, 0.0)
         acc_ref[...] = jnp.zeros((QROWS, LAT), jnp.float32)
     else:
-        high_ref[...] = high_in[...]
-        total_ref[...] = total_in[...]
+        stat_ref[...] = stat_in[...]
         acc_ref[...] = acc_in[...]
     span = blocks * PACK
     rounds = count_ref[base, 0]
     for block in range(1, blocks):
         rounds = jnp.maximum(rounds, count_ref[base + block, 0])
 
-    def one_round(number, carry):
+    def one_round(number):
         absent = []
         for block in range(blocks):
-            left, right = halves[2 * block], halves[2 * block + 1]
             slot = (lax.broadcasted_iota(jnp.int32, (PACK, ROWS), 0) + number * PACK).astype(jnp.float32)
             pick = jnp.where(slot == pos_ref[base + block : base + block + 1, :], 1.0, 0.0).astype(jnp.bfloat16)
-            packed = lax.dot_general(left[...], pick[:, :HALF], NT, preferred_element_type=jnp.float32)
-            packed = packed + lax.dot_general(right[...], pick[:, HALF:], NT, preferred_element_type=jnp.float32)
-            packed_ref[:, block * PACK : (block + 1) * PACK] = packed.astype(jnp.bfloat16)
+            depth = KV // len(sources[block])
+            for number_in, piece in enumerate(sources[block]):
+                packed = lax.dot_general(piece[...], pick, NT, preferred_element_type=jnp.float32)
+                packed_ref[number_in * depth : (number_in + 1) * depth, block * PACK : (block + 1) * PACK] = (
+                    packed.astype(jnp.bfloat16)
+                )
             present = lax.dot_general(
                 mask_ref[base + block].astype(jnp.bfloat16), pick, NT, preferred_element_type=jnp.float32
             )
             absent.append(jnp.where(present > 0.5, 0.0, -jnp.inf))
         absent = jnp.concatenate(absent, axis=1)
+        column = lax.broadcasted_iota(jnp.int32, (QTILE, STAT), 1)
         for part in range(QROWS // QTILE):
             here = slice(part * QTILE, (part + 1) * QTILE)
             scores = jnp.dot(query_ref[here, :], packed_ref[...], preferred_element_type=jnp.float32)
             scores = scores.reshape(QTILE // 64, PAIRS, HEADS, span) * SCORE_SCALE + absent[None, :, None, :]
             scores = scores.reshape(QTILE, span)
-            former = high_ref[here, :1]
+            former = stat_ref[here, :1]
             newer = jnp.maximum(former, jnp.max(scores, axis=1, keepdims=True))
             weights = jnp.exp2(scores - newer)
             decay = jnp.exp2(former - newer)
-            total = total_ref[here, :1] * decay + jnp.sum(weights, axis=1, keepdims=True)
+            total = stat_ref[here, STAT // 2 : STAT // 2 + 1] * decay + jnp.sum(weights, axis=1, keepdims=True)
             added = lax.dot_general(
                 weights.astype(jnp.bfloat16), packed_ref[:LAT, :], NT, preferred_element_type=jnp.float32
             )
             acc_ref[here, :] = acc_ref[here, :] * decay + added
-            high_ref[here, :] = jnp.broadcast_to(newer, (QTILE, STAT))
-            total_ref[here, :] = jnp.broadcast_to(total, (QTILE, STAT))
-        return carry
-
-    lax.fori_loop(0, (rounds + (PACK - 1)) // PACK, one_round, 0)
+            stat_ref[here, :] = jnp.where(column < STAT // 2, newer, total)
+
+    pl.loop(0, (rounds + (PACK - 1)) // PACK)(one_round)
+
     if last:
-        out_ref[:, :LAT] = acc_ref[...].astype(jnp.bfloat16)
-        lane = lax.broadcasted_iota(jnp.int32, (QROWS, STAT), 1)
-        stats = split_three(high_ref[...], lane, 0) + split_three(total_ref[...], lane, 3)
-        out_ref[:, LAT:] = stats.astype(jnp.bfloat16)
-
-
-def attend(base, counts, query_rows, masks, positions, halves, state=None, last=False):
-    blocks = len(halves) // 2
+        column = lax.broadcasted_iota(jnp.int32, (QTILE, STAT), 1)
+        for part in range(QROWS // QTILE):
+            here = slice(part * QTILE, (part + 1) * QTILE)
+            out_ref[here, :LAT] = acc_ref[here, :].astype(jnp.bfloat16)
+            stats = split_three(stat_ref[here, :1], column, 0) + split_three(
+                stat_ref[here, STAT // 2 : STAT // 2 + 1], column, 3
+            )
+            out_ref[here, LAT:] = stats.astype(jnp.bfloat16)
+
+
+def attend(base, counts, query_rows, masks, positions, sources, state=None, last=False):
+    parts = [len(pieces) for pieces in sources]
+    blocks = len(parts)
     first = state is None
     state_shapes = (
-        jax.ShapeDtypeStruct((QROWS, STAT), jnp.float32),
         jax.ShapeDtypeStruct((QROWS, STAT), jnp.float32),
         jax.ShapeDtypeStruct((QROWS, LAT), jnp.float32),
     )
@@ -157,26 +166,26 @@
         scratch = [pltpu.VMEM(s.shape, s.dtype) for s in state_shapes]
     else:
         out_shape = state_shapes
-        out_specs = (vmem(), vmem(), vmem())
+        out_specs = (vmem(), vmem())
         scratch = []
     scratch = scratch + [pltpu.VMEM((KV, blocks * PACK), jnp.bfloat16)]
-    args = [counts, query_rows, masks, positions] + list(halves) + ([] if first else list(state))
+    moved = sum([list(pieces) for pieces in sources], []) + ([] if first else list(state))
 
     def body(*refs):
-        attend_kernel(base, blocks, first, last, *refs)
+        attend_kernel(base, parts, first, last, *refs)
 
     return pl.pallas_call(
         body,
         out_shape=out_shape,
-        in_specs=[smem()] + [vmem()] * (len(args) - 1),
+        in_specs=[smem()] + [vmem()] * (3 + len(moved)),
         out_specs=out_specs,
         scratch_shapes=scratch,
-        compiler_params=pltpu.CompilerParams(vmem_limit_bytes=40 << 20),
+        compiler_params=pltpu.CompilerParams(vmem_limit_bytes=24 << 20),
         cost_estimate=pl.CostEstimate(
             flops=blocks * 2 * PACK * ROWS * (KV + KV + LAT), bytes_accessed=8 << 20, transcendentals=blocks * QROWS * PACK
         ),
         name="attend_%d" % blocks,
-    )(*args)
+    )(counts, query_rows, masks, positions, *moved)
 
 
 def project_kernel(place_ref, recv_ref, value_ref, out_proj_ref, partial_ref, out_ref, weights, sems):
@@ -230,30 +239,30 @@
     return pl.pallas_call(
         project_kernel,
         out_shape=jax.ShapeDtypeStruct((PAIRS, out_proj.shape[1] + STAT), jnp.bfloat16),
-        in_specs=[smem(), vmem(), vmem(), pl.BlockSpec(memory_space=pltpu.HBM), vmem()],
+        in_specs=[smem(), vmem(), vmem(), pl.BlockSpec(memory_space=pl.ANY), vmem()],
         out_specs=vmem(),
         scratch_shapes=[pltpu.VMEM(out_proj.shape, out_proj.dtype), pltpu.SemaphoreType.DMA((PIECES,))],
-        compiler_params=pltpu.CompilerParams(vmem_limit_bytes=60 << 20),
+        compiler_params=pltpu.CompilerParams(vmem_limit_bytes=24 << 20),
         cost_estimate=pl.CostEstimate(flops=2 * 8 * 1024 * 7168, bytes_accessed=18 << 20, transcendentals=0),
         name="project",
-    )(place, received, value_proj, out_proj, partial)
-
-
-def gather_kernel(own_ref, other_ref, unused_low, unused_high, out_ref):
+    )(place, received, value_proj, pltpu.with_memory_space_constraint(out_proj, pltpu.HBM), partial)
+
+
+def gather_kernel(own_ref, other_ref, out_ref):
     out_ref[0] = own_ref[...]
     out_ref[1] = other_ref[...]
 
 
-def paired(own, other, far):
+def paired(own, other):
     return pl.pallas_call(
         gather_kernel,
         out_shape=jax.ShapeDtypeStruct((2,) + own.shape, own.dtype),
-        in_specs=[vmem(), vmem()] + [pl.BlockSpec(memory_space=pl.ANY)] * 2,
+        in_specs=[vmem(), vmem()],
         out_specs=vmem(),
         compiler_params=pltpu.CompilerParams(vmem_limit_bytes=4 << 20),
         cost_estimate=pl.CostEstimate(flops=1000, bytes_accessed=1 << 19, transcendentals=0),
         name="index_pair",
-    )(own, other, *far)
+    )(own, other)
 
 
 def index_kernel(place_ref, here_ref, one_ref, two_ref, three_ref, key_ref, unused_ref, out_ref):
@@ -330,16 +339,19 @@
 
 def final_kernel(own_ref, far_ref, right_ref, left_ref, out_ref, log_ref):
     summed, logs = four_sum((own_ref, far_ref, right_ref, left_ref))
-    out_ref[...] = summed.astype(jnp.bfloat16)
-    log_ref[...] = jnp.broadcast_to(logs, log_ref.shape)
+    steps, local = log_ref.shape
+    flat = jnp.broadcast_to(logs, (PAIRS, STAT)).T[:1, :]
+    for step in range(steps):
+        out_ref[step] = summed[step * local : (step + 1) * local, :].astype(jnp.bfloat16)
+        log_ref[step : step + 1, :] = flat[:, step * local : (step + 1) * local]
 
 
 def summed_over(value, shift, final):
     parts = (value,) + tuple(lax.ppermute(value, "tp", shift(step)) for step in (2, 1, 3))
     if final:
         out_shape = (
-            jax.ShapeDtypeStruct((PAIRS, value.shape[1] - STAT), jnp.bfloat16),
-            jax.ShapeDtypeStruct((PAIRS, STAT), jnp.float32),
+            jax.ShapeDtypeStruct(final + (value.shape[1] - STAT,), jnp.bfloat16),
+            jax.ShapeDtypeStruct(final, jnp.float32),
         )
         out_specs = (vmem(), vmem())
     else:
@@ -354,6 +366,27 @@
         cost_estimate=pl.CostEstimate(flops=1 << 18, bytes_accessed=1 << 19, transcendentals=0),
         name="sum_last" if final else "sum_first",
     )(*parts)
+
+
+def prepare_kernel(latent_ref, query_ref, block_ref, copies_ref):
+    block_ref[...] = latent_ref[...].astype(jnp.bfloat16)
+    for owner in range(TP):
+        copies_ref[owner] = query_ref[...]
+
+
+def prepare(latent, own_queries):
+    return pl.pallas_call(
+        prepare_kernel,
+        out_shape=(
+            jax.ShapeDtypeStruct(latent.shape, jnp.bfloat16),
+            jax.ShapeDtypeStruct((TP,) + own_queries.shape, own_queries.dtype),
+        ),
+        in_specs=[vmem(), vmem()],
+        out_specs=(vmem(), vmem()),
+        compiler_params=pltpu.CompilerParams(vmem_limit_bytes=16 << 20),
+        cost_estimate=pl.CostEstimate(flops=1000, bytes_accessed=5 << 20, transcendentals=0),
+        name="prepare",
+    )(latent, own_queries)
 
 
 def x_shift(step):
@@ -386,24 +419,19 @@
     me_pre = lax.axis_index("pre")
     me_tp = lax.axis_index("tp")
 
-    block = latent_rows.T.astype(jnp.bfloat16)
-    low, high = block[:, :HALF], block[:, HALF:]
-    fwd_low = lax.ppermute(low, "pre", x_shift(1))
-    bwd_high = lax.ppermute(high, "pre", x_shift(3))
-    fwd_high = lax.ppermute(high, "pre", x_shift(1))
-    bwd_low = lax.ppermute(low, "pre", x_shift(3))
-
-    def with_swapped(parts):
-        return parts + [lax.ppermute(part, "pre", CORE_SWAP) for part in parts]
-
-    own_queries = queries.reshape(PAIRS * HEADS, KV)
-    all_queries = lax.all_to_all(
-        jnp.broadcast_to(own_queries[None], (TP, PAIRS * HEADS, KV)), "tp", 0, 0
-    ).reshape(QROWS, KV)
-
-    fwd_low, bwd_high, all_queries = lax.optimization_barrier((fwd_low, bwd_high, all_queries))
-    far_low = lax.ppermute(fwd_low, "pre", x_shift(1))
-    far_high = lax.ppermute(bwd_high, "pre", x_shift(3))
+    block, copies = prepare(latent_rows.T, queries.reshape(PAIRS * HEADS, KV))
+    forward = lax.ppermute(block, "pre", x_shift(1))
+    backward = lax.ppermute(block, "pre", x_shift(3))
+    all_queries = lax.all_to_all(copies, "tp", 0, 0).reshape(QROWS, KV)
+
+    def swapped(part):
+        return lax.ppermute(part, "pre", CORE_SWAP)
+
+    forward, backward, all_queries = lax.optimization_barrier((forward, backward, all_queries))
+    far = [
+        lax.ppermute(forward[: KV // 2], "pre", x_shift(1)),
+        lax.ppermute(backward[KV // 2 :], "pre", x_shift(3)),
+    ]
 
     valid = (jnp.arange(BLOCK, dtype=jnp.int32) < block_count[..., None]) & (block_owner == me_tp)[..., None]
     source = block_rows >> 10
@@ -411,31 +439,24 @@
     effective = jnp.where(valid, (relative << 10) | (block_rows & (ROWS - 1)), -1).reshape(PAIRS, -1)
     masks, positions, counts = make_tables(effective)
 
-    near = with_swapped([fwd_low, fwd_high]) + with_swapped([low, high]) + with_swapped([bwd_low, bwd_high])
+    gate_rows = jnp.pad(index_gates.reshape(4, IDX), ((0, 12), (0, 0)))
+    piece = jnp.concatenate([index_queries.reshape(PAIRS * 64, IDX), gate_rows], axis=0)
+    slab = paired(piece, swapped(piece))
+    slabs = [slab] + [lax.ppermute(slab, "pre", x_shift(4 - step)) for step in (1, 2, 3)]
+    place = jnp.stack([me_pre >> 1, me_pre & 1]).astype(jnp.int32)
+
+    near = [[part] for whole in (forward, block, backward) for part in (whole, swapped(whole))]
     state = attend(0, counts, all_queries, masks, positions, near)
-    far_low, far_high, high, total, acc = lax.optimization_barrier((far_low, far_high) + tuple(state))
-    state = (high, total, acc)
-    far = with_swapped([far_low, far_high])
+    far, slabs, state = lax.optimization_barrier((far, slabs, state))
+    far = [far, [swapped(part) for part in far]]
     payload = attend(6, counts, all_queries, masks, positions, far, state, last=True)
     received = lax.all_to_all(payload.reshape(TP, PAIRS * HEADS, LAT + STAT), "tp", 0, 0)
-
-    gate_rows = jnp.pad(index_gates.reshape(4, IDX), ((0, 12), (0, 0)))
-    piece = jnp.concatenate([index_queries.reshape(PAIRS * 64, IDX), gate_rows], axis=0)
-    slab = paired(piece, lax.ppermute(piece, "pre", CORE_SWAP), far[:2])
-    slabs = [slab] + [lax.ppermute(slab, "pre", x_shift(4 - step)) for step in (1, 2, 3)]
-    place = jnp.stack([me_pre >> 1, me_pre & 1]).astype(jnp.int32)
     partial = index_partial(place, slabs, index_keys, payload)
     partial = log_add(partial, lax.ppermute(partial, "pre", CORE_SWAP))
     parts = [lax.ppermute(partial, "pre", x_shift(step)) for step in (2, 1, 3)]
     partial = log_add(log_add(partial, parts[0]), log_add(parts[1], parts[2]))
     part_out = project(place, received, value_proj, out_proj, partial)
-    attended, index_total = summed_over(summed_over(part_out, y_shift, False), z_shift, True)
-    index_total = index_total[:, 0]
-    steps, queries_local = queries.shape[0], queries.shape[1]
-    return (
-        attended.reshape(steps, queries_local, out_proj.shape[1]),
-        index_total.reshape(steps, queries_local),
-    )
+    return summed_over(summed_over(part_out, y_shift, None), z_shift, queries.shape[:2])
 
 
 def solution(mesh):

time: 139 us -> 132 us (0.950)
  starting transfers between devices: 46.7 us -> 37.8 us
  other arithmetic: 3.72 us -> 0.33 us
  local copies, waits for them, and re-layouts: 6.5 us -> 9.51 us
    ppermute x15 -> x10, waiting for transfers between devices: 24 us -> 2.36 us  [the longest x6 2.35 us: swapped(): return lax.ppermute(part, 'pre', CORE_SWAP)]
    all_to_all x1, waiting for transfers between devices: 0.01 us -> 20 us  [on_device(): all_queries = lax.all_to_all(copies, 'tp', 0, 0).reshape(QROWS, KV)]
    ppermute x3, waiting for transfers between devices: 14.3 us -> 7.48 us  [on_device(): lax.ppermute(slab, 'pre', x_shift(4 - step))]
    all_to_all x1, waiting for transfers between devices: 0.01 us -> 6.64 us  [on_device(): lax.all_to_all(payload.reshape(TP, PAIRS * HEADS, LAT + STAT), 'tp', 0, 0)]
    ppermute x6, starting transfers between devices: 13 us -> 8.64 us  [summed_over(): lax.ppermute(value, 'tp', shift(step))]
    slice x2, local copies, waits for them, and re-layouts: 0.19 us -> 3.86 us  [the longest x1 1.94 us: on_device(): backward[KV // 2:]]
    ppermute x15 -> x10, starting transfers between devices: 11.4 us -> 7.81 us  [the longest x1 2.96 us: on_device(): lax.ppermute(backward[KV // 2:], 'pre', x_shift(3))]
    unnamed x22 -> x30, local copies, waits for them, and re-layouts: 2.61 us -> 5.44 us
  transfers between devices with their start and end apart: 30 -> 25, of which waited for: 16 -> 14; matrix products, arithmetic and copies ran while one was open for 3% -> 3% of each run, Pallas kernels for 13% -> 14%
where the time goes in v1:
time: 132 us; the launch traced here: 130 us
  waiting for transfers between devices  47.9 us (36%)
  starting transfers between devices  37.8 us (29%)
  Pallas kernels  33.9 us (26%)
  local copies, waits for them, and re-layouts  9.51 us (7%)
    all_to_all x1, waiting for transfers between devices, on_device(): all_queries = lax.all_to_all(copies, 'tp', 0, 0).reshape(QROWS, KV)  20 us
    pallas_call x2, Pallas kernels, attend(): pl.pallas_call(body, out_shape=out_shape, in_specs=[smem()] + [vmem()] *...  18.3 us
    ppermute x6, starting transfers between devices, summed_over(): lax.ppermute(value, 'tp', shift(step))  8.64 us
    all_to_all x1, starting transfers between devices, on_device(): all_queries = lax.all_to_all(copies, 'tp', 0, 0).reshape(QROWS, KV)  8.26 us
    ppermute x6, waiting for transfers between devices, summed_over(): lax.ppermute(value, 'tp', shift(step))  7.78 us
    ppermute x3, waiting for transfers between devices, on_device(): lax.ppermute(slab, 'pre', x_shift(4 - step))  7.48 us
    all_to_all x1, waiting for transfers between devices, on_device(): lax.all_to_all(payload.reshape(TP, PAIRS * HEADS, LAT + STAT), 'tp', 0, 0)  6.64 us
    pallas_call x1, Pallas kernels, project(): pl.pallas_call(project_kernel, out_shape=jax.ShapeDtypeStruct((PAIRS, out...  6.42 us
  transfers between devices with their start and end apart: 25, of which 14 were waited for; matrix products, arithmetic and copies ran while one was open for 3% of the time, Pallas kernels for 14%

profile of v1, /device:TPU:0, one launch (start us, length us, event | category | flops | bytes accessed | tf_op | source)
XLA Modules:
  0.0 130.3 jit_solution(9246537391394349438)
XLA Ops:
  0.6 1.7 %copy-done = f32[1024,576]{0,1:T(8,128)S(1)} copy-done((f32[1024,576]{0,1:T(8,128)S(1)}, f32[1024,576]{0,1:T(8,128)}, u32[]{:S(2)}) %copy-start) | copy-done | bytes 2359320
  2.3 0.9 copy-done.2
  3.2 1.5 %prepare.1 = (bf16[576,1024]{1,0:T(8,128)(2,1)}, bf16[16,64,576]{2,1,0:T(8,128)(2,1)}) custom-call(f32[576,1024]{1,0:T(8,128)S(1)} %bitcast.13, bf16[64,576]{1,0:T(8,128)(2,1)S(1)} %bitcast.14), custom_call_target="tpu_custom_call" | custom-call | flops 1000 | bytes 5242880 | tf_op jit(solution)/shard_map/prepare/pallas_call | solution.py:378
  4.7 1.6 %collective-permute-start = (bf16[576,1024]{1,0:T(8,128)(2,1)}, bf16[576,1024]{1,0:T(8,128)(2,1)}, u32[]{:S(2)}, u32[]{:S(2)}) collective-permute-start(bf16[576,1024]{1,0:T(8,128)(2,1)} %get-tuple-element.21.refs_6_), channel_id=1, source_target_pairs={{0,32},{16,48},{32,64},{48,80},{64,96},{80,112},{96,0},{112,16},{1... | collective-permute-start | bytes 3538952 | tf_op jit(solution)/shard_map/ppermute | solution.py:423
  6.3 1.7 %collective-permute-start.1 = (bf16[576,1024]{1,0:T(8,128)(2,1)}, bf16[576,1024]{1,0:T(8,128)(2,1)}, u32[]{:S(2)}, u32[]{:S(2)}) collective-permute-start(bf16[576,1024]{1,0:T(8,128)(2,1)} %get-tuple-element.21.refs_6_), channel_id=1, source_target_pairs={{0,96},{16,112},{32,0},{48,16},{64,32},{80,48},{96,64},{112,80},{1... | collective-permute-start | bytes 3538952 | tf_op jit(solution)/shard_map/ppermute | solution.py:424
  8.0 8.3 %all-to-all-start = ((bf16[16,64,576]{2,1,0:T(8,128)(2,1)}), bf16[16,64,576]{2,1,0:T(8,128)(2,1)S(1)}, u32[]{:S(2)}, u32[]{:S(2)}) async-start(bf16[16,64,576]{2,1,0:T(8,128)(2,1)} %get-tuple-element.22), calls=%async_computation | async-start | bytes 2621440 | tf_op jit(solution)/shard_map/all_to_all | solution.py:425
  16.3 20.0 %all-to-all-done = bf16[16,64,576]{2,1,0:T(8,128)(2,1)S(1)} async-done(((bf16[16,64,576]{2,1,0:T(8,128)(2,1)}), bf16[16,64,576]{2,1,0:T(8,128)(2,1)S(1)}, u32[]{:S(2)}, u32[]{:S(2)}) %all-to-all-start) | async-done | bytes 1179680 | tf_op jit(solution)/shard_map/all_to_all | solution.py:425
  36.4 0.5 collective-permute-start.8
  37.0 0.2 collective-permute-start.4
  37.2 1.9 %slice.6 = bf16[288,1024]{1,0:T(8,128)(2,1)} slice(bf16[576,1024]{1,0:T(8,128)(2,1)} %collective-permute-done.refs_4_), slice={[0:288], [0:1024]} | slice | bytes 1179648 | tf_op jit(solution)/shard_map/slice | solution.py:432
  39.1 1.9 %slice.7 = bf16[288,1024]{1,0:T(8,128)(2,1)} slice(bf16[576,1024]{1,0:T(8,128)(2,1)} %collective-permute-done.1.refs_8_), slice={[288:576], [0:1024]} | slice | bytes 1179648 | tf_op jit(solution)/shard_map/slice | solution.py:433
  41.0 0.3 collective-permute-start.2
  41.3 3.0 %collective-permute-start.3 = (bf16[288,1024]{1,0:T(8,128)(2,1)}, bf16[288,1024]{1,0:T(8,128)(2,1)S(1)}, u32[]{:S(2)}, u32[]{:S(2)}) collective-permute-start(bf16[288,1024]{1,0:T(8,128)(2,1)} %slice.7), channel_id=1, source_target_pairs={{0,96},{16,112},{32,0},{48,16},{64,32},{80,48},{96,64},{112,80},{1... | collective-permute-start | bytes 1769480 | tf_op jit(solution)/shard_map/ppermute | solution.py:433
  44.3 0.2 or_select_fusion
  44.6 3.3 %row_tables.1 = (f32[8,8,1024]{2,1,0:T(8,128)S(1)}, f32[8,1024]{1,0:T(8,128)S(1)}, s32[8,128]{1,0:T(8,128)S(1)}) custom-call(s32[8,4096]{1,0:T(8,128)S(1)} %reshape.24.rows_ref), custom_call_target="tpu_custom_call" | custom-call | flops 536870912 | bytes 524288 | tf_op jit(solution)/shard_map/row_tables/pallas_call | solution.py:66
  48.0 0.4 collective-permute-start.5
  48.4 0.8 collective-permute-start.6
  49.2 1.0 collective-permute-start.7
  50.1 12.1 %attend_6.1 = (f32[1024,128]{1,0:T(8,128)S(1)}, f32[1024,512]{1,0:T(8,128)S(1)}) custom-call(s32[8,128]{1,0:T(8,128)S(1)} %get-tuple-element.20.refs_0_, bf16[1024,576]{1,0:T(8,128)(2,1)S(1)} %bitcast.11, f32[8,8,1024]{2,1,0:T(8,128)S(1)} %get-tuple-element.24.refs_2_, f32[8,1024]{1,0:T(8,128)S(1)} %get-tuple-element.25.refs_3_, ...), custom_call_target="tpu_custom_call" | custom-call | flops 5234491392 | bytes 8388608 | tf_op jit(solution)/shard_map/attend_6/pallas_call | solution.py:177
  62.2 6.8 %collective-permute-done.5.one_ref = bf16[2,528,128]{2,1,0:T(8,128)(2,1)S(1)} collective-permute-done((bf16[2,528,128]{2,1,0:T(8,128)(2,1)S(1)}, bf16[2,528,128]{2,1,0:T(8,128)(2,1)S(1)}, u32[]{:S(2)}, u32[]{:S(2)}) %collective-permute-start.5) | collective-permute-done | bytes 270368 | tf_op jit(solution)/shard_map/ppermute | solution.py:445
  69.0 0.7 collective-permute-done.7.three_ref
  69.8 0.5 collective-permute-start.12
  70.3 1.5 %collective-permute-done.11.refs_6_ = bf16[288,1024]{1,0:T(8,128)(2,1)S(1)} collective-permute-done((bf16[288,1024]{1,0:T(8,128)(2,1)S(1)}, bf16[288,1024]{1,0:T(8,128)(2,1)S(1)}, u32[]{:S(2)}, u32[]{:S(2)}) %collective-permute-start.11) | collective-permute-done | bytes 589856 | tf_op jit(solution)/shard_map/ppermute | solution.py:428
  71.8 0.8 collective-permute-done.12.refs_7_
  72.7 6.2 %attend_2.1.unused_ref = bf16[1024,640]{1,0:T(8,128)(2,1)} custom-call(s32[8,128]{1,0:T(8,128)S(1)} %get-tuple-element.20.refs_0_, bf16[1024,576]{1,0:T(8,128)(2,1)S(1)} %bitcast.12, f32[8,8,1024]{2,1,0:T(8,128)S(1)} %get-tuple-element.24.refs_2_, f32[8,1024]{1,0:T(8,128)S(1)} %get-tuple-element.25.refs_3_, ...), custom_call_target="tpu_custom_call" | custom-call | flops 1744830464 | bytes 8388608 | tf_op jit(solution)/shard_map/attend_2/pallas_call | solution.py:177
  78.8 5.9 %all-to-all-start.1 = ((bf16[16,64,640]{2,1,0:T(8,128)(2,1)}), bf16[16,64,640]{2,1,0:T(8,128)(2,1)S(1)}, u32[]{:S(2)}, u32[]{:S(2)}) async-start(bf16[16,64,640]{2,1,0:T(8,128)(2,1)} %bitcast.6), calls=%async_computation.1 | async-start | bytes 2621440 | tf_op jit(solution)/shard_map/all_to_all | solution.py:453
  84.8 1.0 copy-done.5
  85.7 1.0 copy-done.7
  86.7 1.0 copy-done.9
  87.6 3.2 %index_partial.1 = f32[8,128]{1,0:T(8,128)S(1)} custom-call(s32[2]{0:T(128)S(1)} %pad_add_fusion.place_ref, bf16[2,528,128]{2,1,0:T(8,128)(2,1)S(1)} %index_pair.1.here_ref, bf16[2,528,128]{2,1,0:T(8,128)(2,1)S(1)} %copy-done.5, bf16[2,528,128]{2,1,0:T(8,128)(2,1)S(1)} %copy-done.7, bf16[2,528,128]{2,1,0:T(8,128)(2,1)S(1)} %copy-done.9, ...), custom_call_target="tpu_custom_call" | custom-call | flops 2147483648 | bytes 2097152 | tf_op jit(solution)/shard_map/index_partial/pallas_call | solution.py:295
  90.9 1.2 collective-permute-done.13
  92.1 1.6 %collective-permute-start.14 = (f32[8,128]{1,0:T(8,128)S(1)}, f32[8,128]{1,0:T(8,128)S(1)}, u32[]{:S(2)}, u32[]{:S(2)}) collective-permute-start(f32[8,128]{1,0:T(8,128)S(1)} %log_add_fusion.1), channel_id=1, source_target_pairs={{0,64},{16,80},{32,96},{48,112},{64,0},{80,16},{96,32},{112,48},{1... | collective-permute-start | bytes 12296 | tf_op jit(solution)/shard_map/ppermute | solution.py:456
  93.7 2.3 %collective-permute-start.15 = (f32[8,128]{1,0:T(8,128)S(1)}, f32[8,128]{1,0:T(8,128)S(1)}, u32[]{:S(2)}, u32[]{:S(2)}) collective-permute-start(f32[8,128]{1,0:T(8,128)S(1)} %log_add_fusion.1), channel_id=1, source_target_pairs={{0,32},{16,48},{32,64},{48,80},{64,96},{80,112},{96,0},{112,16},{1... | collective-permute-start | bytes 12296 | tf_op jit(solution)/shard_map/ppermute | solution.py:456
  96.0 1.2 collective-permute-start.16
  97.3 1.5 %collective-permute-done.15 = f32[8,128]{1,0:T(8,128)S(1)} collective-permute-done((f32[8,128]{1,0:T(8,128)S(1)}, f32[8,128]{1,0:T(8,128)S(1)}, u32[]{:S(2)}, u32[]{:S(2)}) %collective-permute-start.15) | collective-permute-done | bytes 4128 | tf_op jit(solution)/shard_map/ppermute | solution.py:456
  98.7 0.9 collective-permute-done.16
  99.6 6.6 %all-to-all-done.1.recv_ref = bf16[16,64,640]{2,1,0:T(8,128)(2,1)S(1)} async-done(((bf16[16,64,640]{2,1,0:T(8,128)(2,1)}), bf16[16,64,640]{2,1,0:T(8,128)(2,1)S(1)}, u32[]{:S(2)}, u32[]{:S(2)}) %all-to-all-start.1) | async-done | bytes 1310752 | tf_op jit(solution)/shard_map/all_to_all | solution.py:453
  106.3 6.4 %project.1.own_ref = bf16[8,7296]{1,0:T(8,128)(2,1)S(1)} custom-call(s32[2]{0:T(128)S(1)} %pad_add_fusion.place_ref, bf16[16,64,640]{2,1,0:T(8,128)(2,1)S(1)} %all-to-all-done.1.recv_ref, bf16[8,512,128]{2,1,0:T(8,128)(2,1)S(1)} %copy-done.1, bf16[1024,7168]{1,0:T(8,128)(2,1)} %out_proj_ref.1, f32[8,128]{1,0:T(8,128)S(1)} %log_add_fusion.partial_ref), custom_call_target="tpu_custom_call" | custom-call | flops 117440512 | bytes 18874368 | tf_op jit(solution)/shard_map/project/pallas_call | solution.py:239
  112.9 3.2 %collective-permute-start.19 = (bf16[8,7296]{1,0:T(8,128)(2,1)S(1)}, bf16[8,7296]{1,0:T(8,128)(2,1)S(1)}, u32[]{:S(2)}, u32[]{:S(2)}) collective-permute-start(bf16[8,7296]{1,0:T(8,128)(2,1)S(1)} %project.1.own_ref), channel_id=1, source_target_pairs={{0,3},{1,0},{2,1},{3,2},{4,7},{5,4},{6,5},{7,6},{8,11},{9,8},{10,9... | collective-permute-start | bytes 350216 | tf_op jit(solution)/shard_map/ppermute | solution.py:350
  116.1 3.1 %collective-permute-done.17.far_ref = bf16[8,7296]{1,0:T(8,128)(2,1)S(1)} collective-permute-done((bf16[8,7296]{1,0:T(8,128)(2,1)S(1)}, bf16[8,7296]{1,0:T(8,128)(2,1)S(1)}, u32[]{:S(2)}, u32[]{:S(2)}) %collective-permute-start.17) | collective-permute-done | bytes 116768 | tf_op jit(solution)/shard_map/ppermute | solution.py:350
  119.2 1.0 collective-permute-done.18.right_ref
  120.3 0.2 sum_first.1.own_ref
  120.5 2.0 %collective-permute-start.20 = (bf16[8,7296]{1,0:T(8,128)(2,1)S(1)}, bf16[8,7296]{1,0:T(8,128)(2,1)S(1)}, u32[]{:S(2)}, u32[]{:S(2)}) collective-permute-start(bf16[8,7296]{1,0:T(8,128)(2,1)S(1)} %sum_first.1.own_ref), channel_id=1, source_target_pairs={{0,8},{1,9},{2,10},{3,11},{4,12},{5,13},{6,14},{7,15},{8,0},{9,1},... | collective-permute-start | bytes 350216 | tf_op jit(solution)/shard_map/ppermute | solution.py:350
  122.5 0.6 collective-permute-start.21
  123.0 2.7 %collective-permute-start.22 = (bf16[8,7296]{1,0:T(8,128)(2,1)S(1)}, bf16[8,7296]{1,0:T(8,128)(2,1)S(1)}, u32[]{:S(2)}, u32[]{:S(2)}) collective-permute-start(bf16[8,7296]{1,0:T(8,128)(2,1)S(1)} %sum_first.1.own_ref), channel_id=1, source_target_pairs={{0,12},{1,13},{2,14},{3,15},{4,0},{5,1},{6,2},{7,3},{8,4},{9,5},{1... | collective-permute-start | bytes 350216 | tf_op jit(solution)/shard_map/ppermute | solution.py:350
  125.7 2.1 %collective-permute-done.20.far_ref = bf16[8,7296]{1,0:T(8,128)(2,1)S(1)} collective-permute-done((bf16[8,7296]{1,0:T(8,128)(2,1)S(1)}, bf16[8,7296]{1,0:T(8,128)(2,1)S(1)}, u32[]{:S(2)}, u32[]{:S(2)}) %collective-permute-start.20) | collective-permute-done | bytes 116768 | tf_op jit(solution)/shard_map/ppermute | solution.py:350
  127.9 1.5 %collective-permute-done.21.right_ref = bf16[8,7296]{1,0:T(8,128)(2,1)S(1)} collective-permute-done((bf16[8,7296]{1,0:T(8,128)(2,1)S(1)}, bf16[8,7296]{1,0:T(8,128)(2,1)S(1)}, u32[]{:S(2)}, u32[]{:S(2)}) %collective-permute-start.21) | collective-permute-done | bytes 116768 | tf_op jit(solution)/shard_map/ppermute | solution.py:350
  129.4 1.0 sum_last.1
  (51 shorter events, 0.9 us)
Async XLA Ops:
  0.6 1.7 %copy-start = (f32[1024,576]{0,1:T(8,128)S(1)}, f32[1024,576]{0,1:T(8,128)}, u32[]{:S(2)}) copy-start(f32[1024,576]{0,1:T(8,128)} %param.10) | copy-start | bytes 7077892
  2.3 0.9 copy-start.2
  4.7 31.6 %collective-permute-start = (bf16[576,1024]{1,0:T(8,128)(2,1)}, bf16[576,1024]{1,0:T(8,128)(2,1)}, u32[]{:S(2)}, u32[]{:S(2)}) collective-permute-start(bf16[576,1024]{1,0:T(8,128)(2,1)} %get-tuple-element.21.refs_6_), channel_id=1, source_target_pairs={{0,32},{16,48},{32,64},{48,80},{64,96},{80,112},{96,0},{112,16},{1... | collective-permute-start | bytes 3538952 | tf_op jit(solution)/shard_map/ppermute | solution.py:423
  6.3 30.1 %collective-permute-start.1 = (bf16[576,1024]{1,0:T(8,128)(2,1)}, bf16[576,1024]{1,0:T(8,128)(2,1)}, u32[]{:S(2)}, u32[]{:S(2)}) collective-permute-start(bf16[576,1024]{1,0:T(8,128)(2,1)} %get-tuple-element.21.refs_6_), channel_id=1, source_target_pairs={{0,96},{16,112},{32,0},{48,16},{64,32},{80,48},{96,64},{112,80},{1... | collective-permute-start | bytes 3538952 | tf_op jit(solution)/shard_map/ppermute | solution.py:424
  8.0 28.9 %copy-start.14 = (bf16[2,4,64]{2,1,0:T(4,128)(2,1)S(1)}, bf16[2,4,64]{2,1,0:T(4,128)(2,1)}, u32[]{:S(2)}) copy-start(bf16[2,4,64]{2,1,0:T(4,128)(2,1)} %param.14) | copy-start | bytes 3076
  8.0 29.0 %copy-start.11 = (bf16[2,4,64,128]{3,2,1,0:T(8,128)(2,1)S(1)}, bf16[2,4,64,128]{3,2,1,0:T(8,128)(2,1)}, u32[]{:S(2)}) copy-start(bf16[2,4,64,128]{3,2,1,0:T(8,128)(2,1)} %param.13) | copy-start | bytes 393220
  8.0 29.2 %copy-start.13 = (s32[2,4,64]{2,1,0:T(4,128)S(1)}, s32[2,4,64]{2,1,0:T(4,128)}, u32[]{:S(2)}) copy-start(s32[2,4,64]{2,1,0:T(4,128)} %param.18) | copy-start | bytes 6148
  8.0 28.4 %all-to-all-start = ((bf16[16,64,576]{2,1,0:T(8,128)(2,1)}), bf16[16,64,576]{2,1,0:T(8,128)(2,1)S(1)}, u32[]{:S(2)}, u32[]{:S(2)}) async-start(bf16[16,64,576]{2,1,0:T(8,128)(2,1)} %get-tuple-element.22), calls=%async_computation | async-start | bytes 2621440 | tf_op jit(solution)/shard_map/all_to_all | solution.py:425
  16.2 31.7 %collective-permute-start.9 = (bf16[576,1024]{1,0:T(8,128)(2,1)}, bf16[576,1024]{1,0:T(8,128)(2,1)}, u32[]{:S(2)}, u32[]{:S(2)}) collective-permute-start(bf16[576,1024]{1,0:T(8,128)(2,1)} %get-tuple-element.21.refs_6_), channel_id=1, source_target_pairs={{0,16},{16,0},{32,48},{48,32},{64,80},{80,64},{96,112},{112,96},{1... | collective-permute-start | bytes 3538952 | tf_op jit(solution)/shard_map/ppermute | solution.py:428
  36.4 12.0 %collective-permute-start.10 = (bf16[576,1024]{1,0:T(8,128)(2,1)}, bf16[576,1024]{1,0:T(8,128)(2,1)}, u32[]{:S(2)}, u32[]{:S(2)}) collective-permute-start(bf16[576,1024]{1,0:T(8,128)(2,1)} %collective-permute-done.1.refs_8_), channel_id=1, source_target_pairs={{0,16},{16,0},{32,48},{48,32},{64,80},{80,64},{96,112},{112,96},{1... | collective-permute-start | bytes 3538952 | tf_op jit(solution)/shard_map/ppermute | solution.py:428
  36.4 12.8 %collective-permute-start.8 = (bf16[576,1024]{1,0:T(8,128)(2,1)}, bf16[576,1024]{1,0:T(8,128)(2,1)}, u32[]{:S(2)}, u32[]{:S(2)}) collective-permute-start(bf16[576,1024]{1,0:T(8,128)(2,1)} %collective-permute-done.refs_4_), channel_id=1, source_target_pairs={{0,16},{16,0},{32,48},{48,32},{64,80},{80,64},{96,112},{112,96},{1... | collective-permute-start | bytes 3538952 | tf_op jit(solution)/shard_map/ppermute | solution.py:428
  37.0 7.3 %copy-start.10 = (s32[2,4,64,64]{3,2,1,0:T(8,128)S(1)}, s32[2,4,64,64]{3,2,1,0:T(8,128)}, u32[]{:S(2)}) copy-start(s32[2,4,64,64]{3,2,1,0:T(8,128)} %param.17) | copy-start | bytes 393220
  37.0 7.3 %copy-start.12 = (s32[2,4,64]{2,1,0:T(4,128)S(1)}, s32[2,4,64]{2,1,0:T(4,128)}, u32[]{:S(2)}) copy-start(s32[2,4,64]{2,1,0:T(4,128)} %param.19) | copy-start | bytes 6148
  37.0 4.3 %collective-permute-start.4 = (bf16[528,128]{1,0:T(8,128)(2,1)S(1)}, bf16[528,128]{1,0:T(8,128)(2,1)S(1)}, u32[]{:S(2)}, u32[]{:S(2)}) collective-permute-start(bf16[528,128]{1,0:T(8,128)(2,1)S(1)} %fusion.2.own_ref), channel_id=1, source_target_pairs={{0,16},{16,0},{32,48},{48,32},{64,80},{80,64},{96,112},{112,96},{1... | collective-permute-start | bytes 405512 | tf_op jit(solution)/shard_map/ppermute | solution.py:428
  41.0 28.7 %collective-permute-start.2 = (bf16[288,1024]{1,0:T(8,128)(2,1)}, bf16[288,1024]{1,0:T(8,128)(2,1)S(1)}, u32[]{:S(2)}, u32[]{:S(2)}) collective-permute-start(bf16[288,1024]{1,0:T(8,128)(2,1)} %slice.6), channel_id=1, source_target_pairs={{0,32},{16,48},{32,64},{48,80},{64,96},{80,112},{96,0},{112,16},{1... | collective-permute-start | bytes 1769480 | tf_op jit(solution)/shard_map/ppermute | solution.py:432
  41.3 28.4 %collective-permute-start.3 = (bf16[288,1024]{1,0:T(8,128)(2,1)}, bf16[288,1024]{1,0:T(8,128)(2,1)S(1)}, u32[]{:S(2)}, u32[]{:S(2)}) collective-permute-start(bf16[288,1024]{1,0:T(8,128)(2,1)} %slice.7), channel_id=1, source_target_pairs={{0,96},{16,112},{32,0},{48,16},{64,32},{80,48},{96,64},{112,80},{1... | collective-permute-start | bytes 1769480 | tf_op jit(solution)/shard_map/ppermute | solution.py:433
  48.0 21.0 %collective-permute-start.5 = (bf16[2,528,128]{2,1,0:T(8,128)(2,1)S(1)}, bf16[2,528,128]{2,1,0:T(8,128)(2,1)S(1)}, u32[]{:S(2)}, u32[]{:S(2)}) collective-permute-start(bf16[2,528,128]{2,1,0:T(8,128)(2,1)S(1)} %index_pair.1.here_ref), channel_id=1, source_target_pairs={{0,96},{16,112},{32,0},{48,16},{64,32},{80,48},{96,64},{112,80},{1... | collective-permute-start | bytes 811016 | tf_op jit(solution)/shard_map/ppermute | solution.py:445
  48.4 20.6 %collective-permute-start.6 = (bf16[2,528,128]{2,1,0:T(8,128)(2,1)S(1)}, bf16[2,528,128]{2,1,0:T(8,128)(2,1)S(1)}, u32[]{:S(2)}, u32[]{:S(2)}) collective-permute-start(bf16[2,528,128]{2,1,0:T(8,128)(2,1)S(1)} %index_pair.1.here_ref), channel_id=1, source_target_pairs={{0,64},{16,80},{32,96},{48,112},{64,0},{80,16},{96,32},{112,48},{1... | collective-permute-start | bytes 811016 | tf_op jit(solution)/shard_map/ppermute | solution.py:445
  49.2 20.5 %collective-permute-start.7 = (bf16[2,528,128]{2,1,0:T(8,128)(2,1)S(1)}, bf16[2,528,128]{2,1,0:T(8,128)(2,1)S(1)}, u32[]{:S(2)}, u32[]{:S(2)}) collective-permute-start(bf16[2,528,128]{2,1,0:T(8,128)(2,1)S(1)} %index_pair.1.here_ref), channel_id=1, source_target_pairs={{0,32},{16,48},{32,64},{48,80},{64,96},{80,112},{96,0},{112,16},{1... | collective-permute-start | bytes 811016 | tf_op jit(solution)/shard_map/ppermute | solution.py:445
  69.0 9.8 %copy-start.4 = (bf16[2,528,128]{2,1,0:T(8,128)(2,1)}, bf16[2,528,128]{2,1,0:T(8,128)(2,1)S(1)}, u32[]{:S(2)}) copy-start(bf16[2,528,128]{2,1,0:T(8,128)(2,1)S(1)} %collective-permute-done.5.one_ref) | copy-start | bytes 811012
  69.0 9.8 %copy-start.6 = (bf16[2,528,128]{2,1,0:T(8,128)(2,1)}, bf16[2,528,128]{2,1,0:T(8,128)(2,1)S(1)}, u32[]{:S(2)}) copy-start(bf16[2,528,128]{2,1,0:T(8,128)(2,1)S(1)} %collective-permute-done.6.two_ref) | copy-start | bytes 811012
  69.7 9.1 %copy-start.8 = (bf16[2,528,128]{2,1,0:T(8,128)(2,1)}, bf16[2,528,128]{2,1,0:T(8,128)(2,1)S(1)}, u32[]{:S(2)}) copy-start(bf16[2,528,128]{2,1,0:T(8,128)(2,1)S(1)} %collective-permute-done.7.three_ref) | copy-start | bytes 811012
  69.7 2.1 %collective-permute-start.11 = (bf16[288,1024]{1,0:T(8,128)(2,1)S(1)}, bf16[288,1024]{1,0:T(8,128)(2,1)S(1)}, u32[]{:S(2)}, u32[]{:S(2)}) collective-permute-start(bf16[288,1024]{1,0:T(8,128)(2,1)S(1)} %collective-permute-done.2.refs_4_), channel_id=1, source_target_pairs={{0,16},{16,0},{32,48},{48,32},{64,80},{80,64},{96,112},{112,96},{1... | collective-permute-start | bytes 1769480 | tf_op jit(solution)/shard_map/ppermute | solution.py:428
  69.8 2.8 %collective-permute-start.12 = (bf16[288,1024]{1,0:T(8,128)(2,1)S(1)}, bf16[288,1024]{1,0:T(8,128)(2,1)S(1)}, u32[]{:S(2)}, u32[]{:S(2)}) collective-permute-start(bf16[288,1024]{1,0:T(8,128)(2,1)S(1)} %collective-permute-done.3.refs_5_), channel_id=1, source_target_pairs={{0,16},{16,0},{32,48},{48,32},{64,80},{80,64},{96,112},{112,96},{1... | collective-permute-start | bytes 1769480 | tf_op jit(solution)/shard_map/ppermute | solution.py:428
  78.8 6.0 %copy-start.3 = (f32[1024,128]{1,0:T(8,128)S(1)}, f32[1024,128]{1,0:T(8,128)}, u32[]{:S(2)}) copy-start(f32[1024,128]{1,0:T(8,128)} %key_ref.1) | copy-start | bytes 1572868
  78.8 27.4 %all-to-all-start.1 = ((bf16[16,64,640]{2,1,0:T(8,128)(2,1)}), bf16[16,64,640]{2,1,0:T(8,128)(2,1)S(1)}, u32[]{:S(2)}, u32[]{:S(2)}) async-start(bf16[16,64,640]{2,1,0:T(8,128)(2,1)} %bitcast.6), calls=%async_computation.1 | async-start | bytes 2621440 | tf_op jit(solution)/shard_map/all_to_all | solution.py:453
  84.8 1.0 copy-start.5
  85.7 1.0 copy-start.7
  86.7 1.0 copy-start.9
  87.6 18.6 %copy-start.1 = (bf16[8,512,128]{2,1,0:T(8,128)(2,1)S(1)}, bf16[8,512,128]{2,1,0:T(8,128)(2,1)}, u32[]{:S(2)}) copy-start(bf16[8,512,128]{2,1,0:T(8,128)(2,1)} %value_ref.1) | copy-start | bytes 3145732
  90.9 1.2 collective-permute-start.13
  92.1 5.2 %collective-permute-start.14 = (f32[8,128]{1,0:T(8,128)S(1)}, f32[8,128]{1,0:T(8,128)S(1)}, u32[]{:S(2)}, u32[]{:S(2)}) collective-permute-start(f32[8,128]{1,0:T(8,128)S(1)} %log_add_fusion.1), channel_id=1, source_target_pairs={{0,64},{16,80},{32,96},{48,112},{64,0},{80,16},{96,32},{112,48},{1... | collective-permute-start | bytes 12296 | tf_op jit(solution)/shard_map/ppermute | solution.py:456
  93.7 5.1 %collective-permute-start.15 = (f32[8,128]{1,0:T(8,128)S(1)}, f32[8,128]{1,0:T(8,128)S(1)}, u32[]{:S(2)}, u32[]{:S(2)}) collective-permute-start(f32[8,128]{1,0:T(8,128)S(1)} %log_add_fusion.1), channel_id=1, source_target_pairs={{0,32},{16,48},{32,64},{48,80},{64,96},{80,112},{96,0},{112,16},{1... | collective-permute-start | bytes 12296 | tf_op jit(solution)/shard_map/ppermute | solution.py:456
  96.0 3.6 %collective-permute-start.16 = (f32[8,128]{1,0:T(8,128)S(1)}, f32[8,128]{1,0:T(8,128)S(1)}, u32[]{:S(2)}, u32[]{:S(2)}) collective-permute-start(f32[8,128]{1,0:T(8,128)S(1)} %log_add_fusion.1), channel_id=1, source_target_pairs={{0,96},{16,112},{32,0},{48,16},{64,32},{80,48},{96,64},{112,80},{1... | collective-permute-start | bytes 12296 | tf_op jit(solution)/shard_map/ppermute | solution.py:456
  112.7 6.5 %collective-permute-start.17 = (bf16[8,7296]{1,0:T(8,128)(2,1)S(1)}, bf16[8,7296]{1,0:T(8,128)(2,1)S(1)}, u32[]{:S(2)}, u32[]{:S(2)}) collective-permute-start(bf16[8,7296]{1,0:T(8,128)(2,1)S(1)} %project.1.own_ref), channel_id=1, source_target_pairs={{0,2},{1,3},{2,0},{3,1},{4,6},{5,7},{6,4},{7,5},{8,10},{9,11},{10,... | collective-permute-start | bytes 350216 | tf_op jit(solution)/shard_map/ppermute | solution.py:350
  112.8 7.5 %collective-permute-start.18 = (bf16[8,7296]{1,0:T(8,128)(2,1)S(1)}, bf16[8,7296]{1,0:T(8,128)(2,1)S(1)}, u32[]{:S(2)}, u32[]{:S(2)}) collective-permute-start(bf16[8,7296]{1,0:T(8,128)(2,1)S(1)} %project.1.own_ref), channel_id=1, source_target_pairs={{0,1},{1,2},{2,3},{3,0},{4,5},{5,6},{6,7},{7,4},{8,9},{9,10},{10,1... | collective-permute-start | bytes 350216 | tf_op jit(solution)/shard_map/ppermute | solution.py:350
  112.9 7.4 %collective-permute-start.19 = (bf16[8,7296]{1,0:T(8,128)(2,1)S(1)}, bf16[8,7296]{1,0:T(8,128)(2,1)S(1)}, u32[]{:S(2)}, u32[]{:S(2)}) collective-permute-start(bf16[8,7296]{1,0:T(8,128)(2,1)S(1)} %project.1.own_ref), channel_id=1, source_target_pairs={{0,3},{1,0},{2,1},{3,2},{4,7},{5,4},{6,5},{7,6},{8,11},{9,8},{10,9... | collective-permute-start | bytes 350216 | tf_op jit(solution)/shard_map/ppermute | solution.py:350
  120.5 7.4 %collective-permute-start.20 = (bf16[8,7296]{1,0:T(8,128)(2,1)S(1)}, bf16[8,7296]{1,0:T(8,128)(2,1)S(1)}, u32[]{:S(2)}, u32[]{:S(2)}) collective-permute-start(bf16[8,7296]{1,0:T(8,128)(2,1)S(1)} %sum_first.1.own_ref), channel_id=1, source_target_pairs={{0,8},{1,9},{2,10},{3,11},{4,12},{5,13},{6,14},{7,15},{8,0},{9,1},... | collective-permute-start | bytes 350216 | tf_op jit(solution)/shard_map/ppermute | solution.py:350
  122.5 6.9 %collective-permute-start.21 = (bf16[8,7296]{1,0:T(8,128)(2,1)S(1)}, bf16[8,7296]{1,0:T(8,128)(2,1)S(1)}, u32[]{:S(2)}, u32[]{:S(2)}) collective-permute-start(bf16[8,7296]{1,0:T(8,128)(2,1)S(1)} %sum_first.1.own_ref), channel_id=1, source_target_pairs={{0,4},{1,5},{2,6},{3,7},{4,8},{5,9},{6,10},{7,11},{8,12},{9,13},{1... | collective-permute-start | bytes 350216 | tf_op jit(solution)/shard_map/ppermute | solution.py:350
  123.0 6.3 %collective-permute-start.22 = (bf16[8,7296]{1,0:T(8,128)(2,1)S(1)}, bf16[8,7296]{1,0:T(8,128)(2,1)S(1)}, u32[]{:S(2)}, u32[]{:S(2)}) collective-permute-start(bf16[8,7296]{1,0:T(8,128)(2,1)S(1)} %sum_first.1.own_ref), channel_id=1, source_target_pairs={{0,12},{1,13},{2,14},{3,15},{4,0},{5,1},{6,2},{7,3},{8,4},{9,5},{1... | collective-permute-start | bytes 350216 | tf_op jit(solution)/shard_map/ppermute | solution.py:350
